TPU v7x, 32 devices: a whole 2x2x4 slice. The times are simulated.
32 devices in a mesh: outer: 8 (over z, x), inner: 4 (over y, core).
Axes of the slice: x: 2, y: 2, z: 4, core: 2. Of those that a mesh axis runs over, the one named last changes fastest.
Arguments:
- queries: bfloat16 [2048, 2048], P(('outer', 'inner')), may hold values from -32 to 32
- keys: bfloat16 [2048, 2048], P(('outer', 'inner')), may hold values from -8 to 8
- values: bfloat16 [2048, 2048], P(('outer', 'inner')), may hold values from -24 to 24
- span_order: int32 [64], P(('outer', 'inner')), may hold values from 0 to 63, each once
Outputs:
- attended: bfloat16 [2048, 2048], P(('outer', 'inner'))
- log_total: float32 [16, 2048], P(None, ('outer', 'inner'))
Inputs may be any that keep to these rules, and one draw needn't show every extreme that they name: `span_order`: a permutation of the span ranks, so positions is a permutation of the rows in which each span of 32 rows holds consecutive ranks in row order.
All inputs are finite; a program needn't handle non-finite values.
Results may differ from a plain program's by a relative error of at most 0.0065.
Values may be sent and summed in bfloat16 or wider, within the bound.
No kernel may reach another device: no remote copies, remote signals or barrier semaphores. Data moves between devices by JAX's collectives and lax.ppermute only.
A program may use at most 64 MiB of HBM per device.

v0:
```python
import math

import jax
import jax.numpy as jnp
from jax import lax
from jax.sharding import PartitionSpec as P

HEADS = 16
HEAD_DIM = 128
SPAN = 32


masked_score = -1e30


def from_behind(array, axis, by):
    length = lax.axis_size(axis)
    return lax.ppermute(array, axis, [(i, (i + by) % length) for i in range(length)])


def attend_block(running, query_tile, query_pos, key_block, value_block, key_pos):
    accumulated, run_max, run_sum = running
    tok_rows = query_tile.shape[0]
    key_count = key_block.shape[0]
    query_heads = query_tile.reshape(tok_rows, HEADS, HEAD_DIM)
    key_heads = key_block.reshape(key_count, HEADS, HEAD_DIM)
    value_heads = value_block.reshape(key_count, HEADS, HEAD_DIM)
    scores = jnp.einsum(
        "qhd,khd->hqk", query_heads, key_heads, preferred_element_type=jnp.float32
    ) * (1.0 / math.sqrt(HEAD_DIM))
    visible = key_pos[None, None, :] <= query_pos[None, :, None]
    scores = jnp.where(visible, scores, masked_score)
    new_max = jnp.maximum(run_max, jnp.max(scores, axis=2))
    weights = jnp.where(visible, jnp.exp(scores - new_max[:, :, None]), 0.0)
    factor = jnp.exp(run_max - new_max)
    new_sum = run_sum * factor + jnp.sum(weights, axis=2)
    update = jnp.einsum(
        "hqk,khd->qhd",
        weights.astype(jnp.bfloat16),
        value_heads,
        preferred_element_type=jnp.float32,
    )
    new_accumulated = accumulated * jnp.transpose(factor)[:, :, None] + update
    return (new_accumulated, new_max, new_sum)


def local(queries, keys, values, span_order):
    tok_rows = queries.shape[0]
    outer_count = lax.axis_size("outer")
    inner_count = lax.axis_size("inner")
    outer_index = lax.axis_index("outer")
    inner_index = lax.axis_index("inner")
    all_spans = lax.all_gather(span_order, ("outer", "inner"), axis=0, tiled=True)
    offsets = jnp.arange(SPAN, dtype=jnp.int32)
    all_pos = (all_spans[:, None] * SPAN + offsets[None, :]).reshape(
        outer_count, inner_count, tok_rows
    )
    key_rows, value_rows = (
        lax.all_gather(keys, "inner", axis=0, tiled=True),
        lax.all_gather(values, "inner", axis=0, tiled=True),
    )
    key_pos = lax.dynamic_index_in_dim(all_pos, outer_index, 0, keepdims=False).reshape(
        inner_count * tok_rows
    )

    def anchor_pos(anchor):
        return lax.dynamic_slice(
            all_pos, (anchor, inner_index, jnp.int32(0)), (1, 1, tok_rows)
        ).reshape(tok_rows)

    def compute(running, query_tile, query_pos):
        return attend_block(running, query_tile, query_pos, key_rows, value_rows, key_pos)

    start_state = (
        jnp.zeros((tok_rows, HEADS, HEAD_DIM), jnp.float32),
        jnp.full((HEADS, tok_rows), masked_score, jnp.float32),
        jnp.zeros((HEADS, tok_rows), jnp.float32),
    )

    def outer_step(turn_index, loop_state):
        query_tile, accumulated, run_max, run_sum = loop_state
        anchor = (outer_index - turn_index) % outer_count
        accumulated, run_max, run_sum = compute(
            (accumulated, run_max, run_sum), query_tile, anchor_pos(anchor)
        )
        query_tile = from_behind(query_tile, "outer", 1)
        accumulated, run_max, run_sum = from_behind((accumulated, run_max, run_sum), "outer", 1)
        return (query_tile, accumulated, run_max, run_sum)

    final_state = lax.fori_loop(0, outer_count, outer_step, (queries,) + start_state)
    accumulated = final_state[1]
    run_max = final_state[2]
    run_sum = final_state[3]
    attended = (
        (accumulated / jnp.transpose(run_sum)[:, :, None])
        .reshape(tok_rows, HEADS * HEAD_DIM)
        .astype(jnp.bfloat16)
    )
    log_total = run_max + jnp.log(run_sum)
    return (attended, log_total)


def solution(mesh):
    return jax.shard_map(
        local,
        mesh=mesh,
        in_specs=(
            P(("outer", "inner"), None),
            P(("outer", "inner"), None),
            P(("outer", "inner"), None),
            P(("outer", "inner")),
        ),
        out_specs=(P(("outer", "inner"), None), P(None, ("outer", "inner"))),
        check_vma=False,
    )
```

profile of v0, /device:TPU:0, one launch (start us, length us, event | category | flops | bytes accessed | tf_op | source)
XLA Modules:
  0.0 228.4 jit_solution(3103843678837461604)
XLA Ops:
  7.2 0.7 all-gather.3.cloned.1.call-update
  7.9 0.7 all-gather.5.cloned.1.call-update
  8.7 0.6 copy-done.3
  9.5 42.0 %all-reduce = s32[64]{0:T(128)S(1)} all-reduce(s32[64]{0:T(128)S(1)} %dynamic-update-slice), channel_id=1, replica_groups=mesh['outer'=8,'inner'=4] {'outer','inner'}, use_global_device_ids=true, to_apply=%add | all-reduce | flops 64 | bytes 512
  52.0 0.5 copy-done.2
  52.5 0.9 copy-done.1
  53.4 166.7 %while.22 = (s32[]{:T(128)}, bf16[64,2048]{1,0:T(8,128)(2,1)S(1)}, f32[64,16,128]{2,0,1:T(8,128)S(1)}, f32[16,64]{1,0:T(8,128)S(1)}, f32[16,64]{1,0:T(8,128)S(1)...) while((s32[]{:T(128)}, bf16[64,2048]{1,0:T(8,128)(2,1)S(1)}, ...), condition=%wide.wide.region_3.4_spmd, body=%wide.wide.region_0.3_spmd.sunk | while | flops 136858640 | bytes 14584052 | solution.py:90
  53.6 1.9 fusion.45
  55.5 0.5 fusion.47
  55.9 2.3 %collective-permute-start.1 = (f32[64,16,128]{2,0,1:T(8,128)S(1)}, f32[64,16,128]{2,0,1:T(8,128)S(1)}, u32[]{:S(2)}, u32[]{:S(2)}) collective-permute-start(f32[64,16,128]{2,0,1:T(8,128)S(1)} %fusion.47), channel_id=1, source_target_pairs={{0,4},{4,8},{8,12},{12,16},{16,20},{20,24},{24,28},{28,0},{1,5},{5... | collective-permute-start | bytes 1572872 | tf_op jit(solution)/shard_map/while/body/eval_jaxpr/ppermute | solution.py:18
  58.3 0.8 collective-permute-start.2
  59.1 2.3 collective-permute-start
  61.8 0.6 collective-permute-start.3
  62.4 11.4 %collective-permute-done.2 = f32[16,64]{1,0:T(8,128)S(1)} collective-permute-done((f32[16,64]{1,0:T(8,128)S(1)}, f32[16,64]{1,0:T(8,128)S(1)}, u32[]{:S(2)}, u32[]{:S(2)}) %collective-permute-start.2) | collective-permute-done | bytes 4128 | tf_op jit(solution)/shard_map/while/body/eval_jaxpr/ppermute | solution.py:18
  73.8 3.7 %collective-permute-done.3 = f32[16,64]{1,0:T(8,128)S(1)} collective-permute-done((f32[16,64]{1,0:T(8,128)S(1)}, f32[16,64]{1,0:T(8,128)S(1)}, u32[]{:S(2)}, u32[]{:S(2)}) %collective-permute-start.3) | collective-permute-done | bytes 4128 | tf_op jit(solution)/shard_map/while/body/eval_jaxpr/ppermute | solution.py:18
  77.7 1.9 fusion.45
  79.6 0.5 fusion.47
  80.1 1.3 collective-permute-start.2
  81.4 0.6 collective-permute-start
  82.4 2.2 collective-permute-start.3
  84.7 13.1 %collective-permute-done.2 = f32[16,64]{1,0:T(8,128)S(1)} collective-permute-done((f32[16,64]{1,0:T(8,128)S(1)}, f32[16,64]{1,0:T(8,128)S(1)}, u32[]{:S(2)}, u32[]{:S(2)}) %collective-permute-start.2) | collective-permute-done | bytes 4128 | tf_op jit(solution)/shard_map/while/body/eval_jaxpr/ppermute | solution.py:18
  97.7 2.9 %collective-permute-done.3 = f32[16,64]{1,0:T(8,128)S(1)} collective-permute-done((f32[16,64]{1,0:T(8,128)S(1)}, f32[16,64]{1,0:T(8,128)S(1)}, u32[]{:S(2)}, u32[]{:S(2)}) %collective-permute-start.3) | collective-permute-done | bytes 4128 | tf_op jit(solution)/shard_map/while/body/eval_jaxpr/ppermute | solution.py:18
  100.8 1.9 fusion.45
  102.7 0.5 fusion.47
  103.8 2.2 collective-permute-start.3
  106.1 13.9 %collective-permute-done.2 = f32[16,64]{1,0:T(8,128)S(1)} collective-permute-done((f32[16,64]{1,0:T(8,128)S(1)}, f32[16,64]{1,0:T(8,128)S(1)}, u32[]{:S(2)}, u32[]{:S(2)}) %collective-permute-start.2) | collective-permute-done | bytes 4128 | tf_op jit(solution)/shard_map/while/body/eval_jaxpr/ppermute | solution.py:18
  120.0 2.9 %collective-permute-done.3 = f32[16,64]{1,0:T(8,128)S(1)} collective-permute-done((f32[16,64]{1,0:T(8,128)S(1)}, f32[16,64]{1,0:T(8,128)S(1)}, u32[]{:S(2)}, u32[]{:S(2)}) %collective-permute-start.3) | collective-permute-done | bytes 4128 | tf_op jit(solution)/shard_map/while/body/eval_jaxpr/ppermute | solution.py:18
  123.0 1.9 fusion.45
  126.0 0.5 collective-permute-start.3
  126.5 14.7 %collective-permute-done.2 = f32[16,64]{1,0:T(8,128)S(1)} collective-permute-done((f32[16,64]{1,0:T(8,128)S(1)}, f32[16,64]{1,0:T(8,128)S(1)}, u32[]{:S(2)}, u32[]{:S(2)}) %collective-permute-start.2) | collective-permute-done | bytes 4128 | tf_op jit(solution)/shard_map/while/body/eval_jaxpr/ppermute | solution.py:18
  141.2 2.9 %collective-permute-done.3 = f32[16,64]{1,0:T(8,128)S(1)} collective-permute-done((f32[16,64]{1,0:T(8,128)S(1)}, f32[16,64]{1,0:T(8,128)S(1)}, u32[]{:S(2)}, u32[]{:S(2)}) %collective-permute-start.3) | collective-permute-done | bytes 4128 | tf_op jit(solution)/shard_map/while/body/eval_jaxpr/ppermute | solution.py:18
  144.3 1.9 fusion.45
  147.4 14.2 %collective-permute-done.2 = f32[16,64]{1,0:T(8,128)S(1)} collective-permute-done((f32[16,64]{1,0:T(8,128)S(1)}, f32[16,64]{1,0:T(8,128)S(1)}, u32[]{:S(2)}, u32[]{:S(2)}) %collective-permute-start.2) | collective-permute-done | bytes 4128 | tf_op jit(solution)/shard_map/while/body/eval_jaxpr/ppermute | solution.py:18
  161.6 2.9 %collective-permute-done.3 = f32[16,64]{1,0:T(8,128)S(1)} collective-permute-done((f32[16,64]{1,0:T(8,128)S(1)}, f32[16,64]{1,0:T(8,128)S(1)}, u32[]{:S(2)}, u32[]{:S(2)}) %collective-permute-start.3) | collective-permute-done | bytes 4128 | tf_op jit(solution)/shard_map/while/body/eval_jaxpr/ppermute | solution.py:18
  164.7 1.9 fusion.45
  166.6 0.5 fusion.47
  167.7 13.3 %collective-permute-done.2 = f32[16,64]{1,0:T(8,128)S(1)} collective-permute-done((f32[16,64]{1,0:T(8,128)S(1)}, f32[16,64]{1,0:T(8,128)S(1)}, u32[]{:S(2)}, u32[]{:S(2)}) %collective-permute-start.2) | collective-permute-done | bytes 4128 | tf_op jit(solution)/shard_map/while/body/eval_jaxpr/ppermute | solution.py:18
  181.1 2.9 %collective-permute-done.3 = f32[16,64]{1,0:T(8,128)S(1)} collective-permute-done((f32[16,64]{1,0:T(8,128)S(1)}, f32[16,64]{1,0:T(8,128)S(1)}, u32[]{:S(2)}, u32[]{:S(2)}) %collective-permute-start.3) | collective-permute-done | bytes 4128 | tf_op jit(solution)/shard_map/while/body/eval_jaxpr/ppermute | solution.py:18
  184.1 1.9 fusion.45
  186.0 0.5 fusion.47
  187.2 12.4 %collective-permute-done.2 = f32[16,64]{1,0:T(8,128)S(1)} collective-permute-done((f32[16,64]{1,0:T(8,128)S(1)}, f32[16,64]{1,0:T(8,128)S(1)}, u32[]{:S(2)}, u32[]{:S(2)}) %collective-permute-start.2) | collective-permute-done | bytes 4128 | tf_op jit(solution)/shard_map/while/body/eval_jaxpr/ppermute | solution.py:18
  199.6 2.9 %collective-permute-done.3 = f32[16,64]{1,0:T(8,128)S(1)} collective-permute-done((f32[16,64]{1,0:T(8,128)S(1)}, f32[16,64]{1,0:T(8,128)S(1)}, u32[]{:S(2)}, u32[]{:S(2)}) %collective-permute-start.3) | collective-permute-done | bytes 4128 | tf_op jit(solution)/shard_map/while/body/eval_jaxpr/ppermute | solution.py:18
  202.6 1.9 fusion.45
  204.5 0.5 fusion.47
  205.7 11.5 %collective-permute-done.2 = f32[16,64]{1,0:T(8,128)S(1)} collective-permute-done((f32[16,64]{1,0:T(8,128)S(1)}, f32[16,64]{1,0:T(8,128)S(1)}, u32[]{:S(2)}, u32[]{:S(2)}) %collective-permute-start.2) | collective-permute-done | bytes 4128 | tf_op jit(solution)/shard_map/while/body/eval_jaxpr/ppermute | solution.py:18
  217.2 2.9 %collective-permute-done.3 = f32[16,64]{1,0:T(8,128)S(1)} collective-permute-done((f32[16,64]{1,0:T(8,128)S(1)}, f32[16,64]{1,0:T(8,128)S(1)}, u32[]{:S(2)}, u32[]{:S(2)}) %collective-permute-start.3) | collective-permute-done | bytes 4128 | tf_op jit(solution)/shard_map/while/body/eval_jaxpr/ppermute | solution.py:18
  220.1 0.6 log_add_fusion
  220.7 0.9 copy_bitcast_fusion
  (134 shorter events, 7.5 us)
Async XLA Ops:
  7.2 45.3 %all-gather.3.cloned.1.call-start = ((), (), s32[]{:S(2)}) async-start(), calls=%async_computation | async-start | bytes 1310720 | tf_op jit(solution)/shard_map/all_gather | solution.py:59
  7.9 44.6 %all-gather.5.cloned.1.call-start = ((), (), s32[]{:S(2)}) async-start(), calls=%async_computation.1 | async-start | bytes 1310720 | tf_op jit(solution)/shard_map/all_gather | solution.py:60
  8.7 0.7 copy-start.3
  51.9 0.6 copy-start.2
  52.5 0.9 copy-start.1
  53.6 1.9 copy-start
  55.9 21.6 %collective-permute-start.1 = (f32[64,16,128]{2,0,1:T(8,128)S(1)}, f32[64,16,128]{2,0,1:T(8,128)S(1)}, u32[]{:S(2)}, u32[]{:S(2)}) collective-permute-start(f32[64,16,128]{2,0,1:T(8,128)S(1)} %fusion.47), channel_id=1, source_target_pairs={{0,4},{4,8},{8,12},{12,16},{16,20},{20,24},{24,28},{28,0},{1,5},{5... | collective-permute-start | bytes 1572872 | tf_op jit(solution)/shard_map/while/body/eval_jaxpr/ppermute | solution.py:18
  58.3 15.5 %collective-permute-start.2 = (f32[16,64]{1,0:T(8,128)S(1)}, f32[16,64]{1,0:T(8,128)S(1)}, u32[]{:S(2)}, u32[]{:S(2)}) collective-permute-start(f32[16,64]{1,0:T(8,128)S(1)} %get-tuple-element.429), channel_id=1, source_target_pairs={{0,4},{4,8},{8,12},{12,16},{16,20},{20,24},{24,28},{28,0},{1,5},{5... | collective-permute-start | bytes 12296 | tf_op jit(solution)/shard_map/while/body/eval_jaxpr/ppermute | solution.py:18
  59.1 18.5 %collective-permute-start = (bf16[64,2048]{1,0:T(8,128)(2,1)S(1)}, bf16[64,2048]{1,0:T(8,128)(2,1)S(1)}, u32[]{:S(2)}, u32[]{:S(2)}) collective-permute-start(bf16[64,2048]{1,0:T(8,128)(2,1)S(1)} %copy.51), channel_id=1, source_target_pairs={{0,4},{4,8},{8,12},{12,16},{16,20},{20,24},{24,28},{28,0},{1,5},{5... | collective-permute-start | bytes 786440 | tf_op jit(solution)/shard_map/while/body/eval_jaxpr/ppermute | solution.py:18
  61.8 15.7 %collective-permute-start.3 = (f32[16,64]{1,0:T(8,128)S(1)}, f32[16,64]{1,0:T(8,128)S(1)}, u32[]{:S(2)}, u32[]{:S(2)}) collective-permute-start(f32[16,64]{1,0:T(8,128)S(1)} %multiply_add_fusion.3), channel_id=1, source_target_pairs={{0,4},{4,8},{8,12},{12,16},{16,20},{20,24},{24,28},{28,0},{1,5},{5... | collective-permute-start | bytes 12296 | tf_op jit(solution)/shard_map/while/body/eval_jaxpr/ppermute | solution.py:18
  77.6 1.9 copy-start
  80.0 20.6 %collective-permute-start.1 = (f32[64,16,128]{2,0,1:T(8,128)S(1)}, f32[64,16,128]{2,0,1:T(8,128)S(1)}, u32[]{:S(2)}, u32[]{:S(2)}) collective-permute-start(f32[64,16,128]{2,0,1:T(8,128)S(1)} %fusion.47), channel_id=1, source_target_pairs={{0,4},{4,8},{8,12},{12,16},{16,20},{20,24},{24,28},{28,0},{1,5},{5... | collective-permute-start | bytes 1572872 | tf_op jit(solution)/shard_map/while/body/eval_jaxpr/ppermute | solution.py:18
  80.1 17.6 %collective-permute-start.2 = (f32[16,64]{1,0:T(8,128)S(1)}, f32[16,64]{1,0:T(8,128)S(1)}, u32[]{:S(2)}, u32[]{:S(2)}) collective-permute-start(f32[16,64]{1,0:T(8,128)S(1)} %get-tuple-element.429), channel_id=1, source_target_pairs={{0,4},{4,8},{8,12},{12,16},{16,20},{20,24},{24,28},{28,0},{1,5},{5... | collective-permute-start | bytes 12296 | tf_op jit(solution)/shard_map/while/body/eval_jaxpr/ppermute | solution.py:18
  81.4 19.3 %collective-permute-start = (bf16[64,2048]{1,0:T(8,128)(2,1)S(1)}, bf16[64,2048]{1,0:T(8,128)(2,1)S(1)}, u32[]{:S(2)}, u32[]{:S(2)}) collective-permute-start(bf16[64,2048]{1,0:T(8,128)(2,1)S(1)} %copy.51), channel_id=1, source_target_pairs={{0,4},{4,8},{8,12},{12,16},{16,20},{20,24},{24,28},{28,0},{1,5},{5... | collective-permute-start | bytes 786440 | tf_op jit(solution)/shard_map/while/body/eval_jaxpr/ppermute | solution.py:18
  82.4 18.2 %collective-permute-start.3 = (f32[16,64]{1,0:T(8,128)S(1)}, f32[16,64]{1,0:T(8,128)S(1)}, u32[]{:S(2)}, u32[]{:S(2)}) collective-permute-start(f32[16,64]{1,0:T(8,128)S(1)} %multiply_add_fusion.3), channel_id=1, source_target_pairs={{0,4},{4,8},{8,12},{12,16},{16,20},{20,24},{24,28},{28,0},{1,5},{5... | collective-permute-start | bytes 12296 | tf_op jit(solution)/shard_map/while/body/eval_jaxpr/ppermute | solution.py:18
  100.8 1.9 copy-start
  103.2 19.7 %collective-permute-start.1 = (f32[64,16,128]{2,0,1:T(8,128)S(1)}, f32[64,16,128]{2,0,1:T(8,128)S(1)}, u32[]{:S(2)}, u32[]{:S(2)}) collective-permute-start(f32[64,16,128]{2,0,1:T(8,128)S(1)} %fusion.47), channel_id=1, source_target_pairs={{0,4},{4,8},{8,12},{12,16},{16,20},{20,24},{24,28},{28,0},{1,5},{5... | collective-permute-start | bytes 1572872 | tf_op jit(solution)/shard_map/while/body/eval_jaxpr/ppermute | solution.py:18
  103.2 16.7 %collective-permute-start.2 = (f32[16,64]{1,0:T(8,128)S(1)}, f32[16,64]{1,0:T(8,128)S(1)}, u32[]{:S(2)}, u32[]{:S(2)}) collective-permute-start(f32[16,64]{1,0:T(8,128)S(1)} %get-tuple-element.429), channel_id=1, source_target_pairs={{0,4},{4,8},{8,12},{12,16},{16,20},{20,24},{24,28},{28,0},{1,5},{5... | collective-permute-start | bytes 12296 | tf_op jit(solution)/shard_map/while/body/eval_jaxpr/ppermute | solution.py:18
  103.3 19.6 %collective-permute-start = (bf16[64,2048]{1,0:T(8,128)(2,1)S(1)}, bf16[64,2048]{1,0:T(8,128)(2,1)S(1)}, u32[]{:S(2)}, u32[]{:S(2)}) collective-permute-start(bf16[64,2048]{1,0:T(8,128)(2,1)S(1)} %copy.51), channel_id=1, source_target_pairs={{0,4},{4,8},{8,12},{12,16},{16,20},{20,24},{24,28},{28,0},{1,5},{5... | collective-permute-start | bytes 786440 | tf_op jit(solution)/shard_map/while/body/eval_jaxpr/ppermute | solution.py:18
  103.8 19.0 %collective-permute-start.3 = (f32[16,64]{1,0:T(8,128)S(1)}, f32[16,64]{1,0:T(8,128)S(1)}, u32[]{:S(2)}, u32[]{:S(2)}) collective-permute-start(f32[16,64]{1,0:T(8,128)S(1)} %multiply_add_fusion.3), channel_id=1, source_target_pairs={{0,4},{4,8},{8,12},{12,16},{16,20},{20,24},{24,28},{28,0},{1,5},{5... | collective-permute-start | bytes 12296 | tf_op jit(solution)/shard_map/while/body/eval_jaxpr/ppermute | solution.py:18
  123.0 1.9 copy-start
  125.4 18.8 %collective-permute-start.1 = (f32[64,16,128]{2,0,1:T(8,128)S(1)}, f32[64,16,128]{2,0,1:T(8,128)S(1)}, u32[]{:S(2)}, u32[]{:S(2)}) collective-permute-start(f32[64,16,128]{2,0,1:T(8,128)S(1)} %fusion.47), channel_id=1, source_target_pairs={{0,4},{4,8},{8,12},{12,16},{16,20},{20,24},{24,28},{28,0},{1,5},{5... | collective-permute-start | bytes 1572872 | tf_op jit(solution)/shard_map/while/body/eval_jaxpr/ppermute | solution.py:18
  125.4 15.8 %collective-permute-start.2 = (f32[16,64]{1,0:T(8,128)S(1)}, f32[16,64]{1,0:T(8,128)S(1)}, u32[]{:S(2)}, u32[]{:S(2)}) collective-permute-start(f32[16,64]{1,0:T(8,128)S(1)} %get-tuple-element.429), channel_id=1, source_target_pairs={{0,4},{4,8},{8,12},{12,16},{16,20},{20,24},{24,28},{28,0},{1,5},{5... | collective-permute-start | bytes 12296 | tf_op jit(solution)/shard_map/while/body/eval_jaxpr/ppermute | solution.py:18
  125.5 18.6 %collective-permute-start = (bf16[64,2048]{1,0:T(8,128)(2,1)S(1)}, bf16[64,2048]{1,0:T(8,128)(2,1)S(1)}, u32[]{:S(2)}, u32[]{:S(2)}) collective-permute-start(bf16[64,2048]{1,0:T(8,128)(2,1)S(1)} %copy.51), channel_id=1, source_target_pairs={{0,4},{4,8},{8,12},{12,16},{16,20},{20,24},{24,28},{28,0},{1,5},{5... | collective-permute-start | bytes 786440 | tf_op jit(solution)/shard_map/while/body/eval_jaxpr/ppermute | solution.py:18
  126.0 18.1 %collective-permute-start.3 = (f32[16,64]{1,0:T(8,128)S(1)}, f32[16,64]{1,0:T(8,128)S(1)}, u32[]{:S(2)}, u32[]{:S(2)}) collective-permute-start(f32[16,64]{1,0:T(8,128)S(1)} %multiply_add_fusion.3), channel_id=1, source_target_pairs={{0,4},{4,8},{8,12},{12,16},{16,20},{20,24},{24,28},{28,0},{1,5},{5... | collective-permute-start | bytes 12296 | tf_op jit(solution)/shard_map/while/body/eval_jaxpr/ppermute | solution.py:18
  144.3 1.9 copy-start
  146.7 17.8 %collective-permute-start.1 = (f32[64,16,128]{2,0,1:T(8,128)S(1)}, f32[64,16,128]{2,0,1:T(8,128)S(1)}, u32[]{:S(2)}, u32[]{:S(2)}) collective-permute-start(f32[64,16,128]{2,0,1:T(8,128)S(1)} %fusion.47), channel_id=1, source_target_pairs={{0,4},{4,8},{8,12},{12,16},{16,20},{20,24},{24,28},{28,0},{1,5},{5... | collective-permute-start | bytes 1572872 | tf_op jit(solution)/shard_map/while/body/eval_jaxpr/ppermute | solution.py:18
  146.7 14.9 %collective-permute-start.2 = (f32[16,64]{1,0:T(8,128)S(1)}, f32[16,64]{1,0:T(8,128)S(1)}, u32[]{:S(2)}, u32[]{:S(2)}) collective-permute-start(f32[16,64]{1,0:T(8,128)S(1)} %get-tuple-element.429), channel_id=1, source_target_pairs={{0,4},{4,8},{8,12},{12,16},{16,20},{20,24},{24,28},{28,0},{1,5},{5... | collective-permute-start | bytes 12296 | tf_op jit(solution)/shard_map/while/body/eval_jaxpr/ppermute | solution.py:18
  146.8 17.7 %collective-permute-start = (bf16[64,2048]{1,0:T(8,128)(2,1)S(1)}, bf16[64,2048]{1,0:T(8,128)(2,1)S(1)}, u32[]{:S(2)}, u32[]{:S(2)}) collective-permute-start(bf16[64,2048]{1,0:T(8,128)(2,1)S(1)} %copy.51), channel_id=1, source_target_pairs={{0,4},{4,8},{8,12},{12,16},{16,20},{20,24},{24,28},{28,0},{1,5},{5... | collective-permute-start | bytes 786440 | tf_op jit(solution)/shard_map/while/body/eval_jaxpr/ppermute | solution.py:18
  147.3 17.2 %collective-permute-start.3 = (f32[16,64]{1,0:T(8,128)S(1)}, f32[16,64]{1,0:T(8,128)S(1)}, u32[]{:S(2)}, u32[]{:S(2)}) collective-permute-start(f32[16,64]{1,0:T(8,128)S(1)} %multiply_add_fusion.3), channel_id=1, source_target_pairs={{0,4},{4,8},{8,12},{12,16},{16,20},{20,24},{24,28},{28,0},{1,5},{5... | collective-permute-start | bytes 12296 | tf_op jit(solution)/shard_map/while/body/eval_jaxpr/ppermute | solution.py:18
  164.6 1.9 copy-start
  167.0 16.9 %collective-permute-start.1 = (f32[64,16,128]{2,0,1:T(8,128)S(1)}, f32[64,16,128]{2,0,1:T(8,128)S(1)}, u32[]{:S(2)}, u32[]{:S(2)}) collective-permute-start(f32[64,16,128]{2,0,1:T(8,128)S(1)} %fusion.47), channel_id=1, source_target_pairs={{0,4},{4,8},{8,12},{12,16},{16,20},{20,24},{24,28},{28,0},{1,5},{5... | collective-permute-start | bytes 1572872 | tf_op jit(solution)/shard_map/while/body/eval_jaxpr/ppermute | solution.py:18
  167.1 14.0 %collective-permute-start.2 = (f32[16,64]{1,0:T(8,128)S(1)}, f32[16,64]{1,0:T(8,128)S(1)}, u32[]{:S(2)}, u32[]{:S(2)}) collective-permute-start(f32[16,64]{1,0:T(8,128)S(1)} %get-tuple-element.429), channel_id=1, source_target_pairs={{0,4},{4,8},{8,12},{12,16},{16,20},{20,24},{24,28},{28,0},{1,5},{5... | collective-permute-start | bytes 12296 | tf_op jit(solution)/shard_map/while/body/eval_jaxpr/ppermute | solution.py:18
  167.2 16.8 %collective-permute-start = (bf16[64,2048]{1,0:T(8,128)(2,1)S(1)}, bf16[64,2048]{1,0:T(8,128)(2,1)S(1)}, u32[]{:S(2)}, u32[]{:S(2)}) collective-permute-start(bf16[64,2048]{1,0:T(8,128)(2,1)S(1)} %copy.51), channel_id=1, source_target_pairs={{0,4},{4,8},{8,12},{12,16},{16,20},{20,24},{24,28},{28,0},{1,5},{5... | collective-permute-start | bytes 786440 | tf_op jit(solution)/shard_map/while/body/eval_jaxpr/ppermute | solution.py:18
  167.7 16.3 %collective-permute-start.3 = (f32[16,64]{1,0:T(8,128)S(1)}, f32[16,64]{1,0:T(8,128)S(1)}, u32[]{:S(2)}, u32[]{:S(2)}) collective-permute-start(f32[16,64]{1,0:T(8,128)S(1)} %multiply_add_fusion.3), channel_id=1, source_target_pairs={{0,4},{4,8},{8,12},{12,16},{16,20},{20,24},{24,28},{28,0},{1,5},{5... | collective-permute-start | bytes 12296 | tf_op jit(solution)/shard_map/while/body/eval_jaxpr/ppermute | solution.py:18
  184.1 1.9 copy-start
  186.5 16.0 %collective-permute-start.1 = (f32[64,16,128]{2,0,1:T(8,128)S(1)}, f32[64,16,128]{2,0,1:T(8,128)S(1)}, u32[]{:S(2)}, u32[]{:S(2)}) collective-permute-start(f32[64,16,128]{2,0,1:T(8,128)S(1)} %fusion.47), channel_id=1, source_target_pairs={{0,4},{4,8},{8,12},{12,16},{16,20},{20,24},{24,28},{28,0},{1,5},{5... | collective-permute-start | bytes 1572872 | tf_op jit(solution)/shard_map/while/body/eval_jaxpr/ppermute | solution.py:18
  186.5 13.0 %collective-permute-start.2 = (f32[16,64]{1,0:T(8,128)S(1)}, f32[16,64]{1,0:T(8,128)S(1)}, u32[]{:S(2)}, u32[]{:S(2)}) collective-permute-start(f32[16,64]{1,0:T(8,128)S(1)} %get-tuple-element.429), channel_id=1, source_target_pairs={{0,4},{4,8},{8,12},{12,16},{16,20},{20,24},{24,28},{28,0},{1,5},{5... | collective-permute-start | bytes 12296 | tf_op jit(solution)/shard_map/while/body/eval_jaxpr/ppermute | solution.py:18
  186.6 15.9 %collective-permute-start = (bf16[64,2048]{1,0:T(8,128)(2,1)S(1)}, bf16[64,2048]{1,0:T(8,128)(2,1)S(1)}, u32[]{:S(2)}, u32[]{:S(2)}) collective-permute-start(bf16[64,2048]{1,0:T(8,128)(2,1)S(1)} %copy.51), channel_id=1, source_target_pairs={{0,4},{4,8},{8,12},{12,16},{16,20},{20,24},{24,28},{28,0},{1,5},{5... | collective-permute-start | bytes 786440 | tf_op jit(solution)/shard_map/while/body/eval_jaxpr/ppermute | solution.py:18
  187.1 15.4 %collective-permute-start.3 = (f32[16,64]{1,0:T(8,128)S(1)}, f32[16,64]{1,0:T(8,128)S(1)}, u32[]{:S(2)}, u32[]{:S(2)}) collective-permute-start(f32[16,64]{1,0:T(8,128)S(1)} %multiply_add_fusion.3), channel_id=1, source_target_pairs={{0,4},{4,8},{8,12},{12,16},{16,20},{20,24},{24,28},{28,0},{1,5},{5... | collective-permute-start | bytes 12296 | tf_op jit(solution)/shard_map/while/body/eval_jaxpr/ppermute | solution.py:18
  202.6 1.9 copy-start
  205.0 15.1 %collective-permute-start.1 = (f32[64,16,128]{2,0,1:T(8,128)S(1)}, f32[64,16,128]{2,0,1:T(8,128)S(1)}, u32[]{:S(2)}, u32[]{:S(2)}) collective-permute-start(f32[64,16,128]{2,0,1:T(8,128)S(1)} %fusion.47), channel_id=1, source_target_pairs={{0,4},{4,8},{8,12},{12,16},{16,20},{20,24},{24,28},{28,0},{1,5},{5... | collective-permute-start | bytes 1572872 | tf_op jit(solution)/shard_map/while/body/eval_jaxpr/ppermute | solution.py:18
  205.1 12.1 %collective-permute-start.2 = (f32[16,64]{1,0:T(8,128)S(1)}, f32[16,64]{1,0:T(8,128)S(1)}, u32[]{:S(2)}, u32[]{:S(2)}) collective-permute-start(f32[16,64]{1,0:T(8,128)S(1)} %get-tuple-element.429), channel_id=1, source_target_pairs={{0,4},{4,8},{8,12},{12,16},{16,20},{20,24},{24,28},{28,0},{1,5},{5... | collective-permute-start | bytes 12296 | tf_op jit(solution)/shard_map/while/body/eval_jaxpr/ppermute | solution.py:18
  205.1 14.9 %collective-permute-start = (bf16[64,2048]{1,0:T(8,128)(2,1)S(1)}, bf16[64,2048]{1,0:T(8,128)(2,1)S(1)}, u32[]{:S(2)}, u32[]{:S(2)}) collective-permute-start(bf16[64,2048]{1,0:T(8,128)(2,1)S(1)} %copy.51), channel_id=1, source_target_pairs={{0,4},{4,8},{8,12},{12,16},{16,20},{20,24},{24,28},{28,0},{1,5},{5... | collective-permute-start | bytes 786440 | tf_op jit(solution)/shard_map/while/body/eval_jaxpr/ppermute | solution.py:18
  205.6 14.4 %collective-permute-start.3 = (f32[16,64]{1,0:T(8,128)S(1)}, f32[16,64]{1,0:T(8,128)S(1)}, u32[]{:S(2)}, u32[]{:S(2)}) collective-permute-start(f32[16,64]{1,0:T(8,128)S(1)} %multiply_add_fusion.3), channel_id=1, source_target_pairs={{0,4},{4,8},{8,12},{12,16},{16,20},{20,24},{24,28},{28,0},{1,5},{5... | collective-permute-start | bytes 12296 | tf_op jit(solution)/shard_map/while/body/eval_jaxpr/ppermute | solution.py:18
Sparse Core Ops, SparseCore 0:
  9.6 19.5 all-gather.2
  30.7 16.7 all-gather.4
where the time goes:
time: 229 us; the launch traced here: 228 us
  waiting for transfers between devices  130 us (57%)
  blocking collectives  42 us (18%)
  matrix products  18.7 us (8%)
  starting transfers between devices  14.3 us (6%)
  between operations  14.1 us (6%)
  other arithmetic  5.65 us (2%)
  local copies, waits for them, and re-layouts  3.01 us (1%)
    ppermute x32, waiting for transfers between devices, from_behind(): lax.ppermute(array, axis, [(i, (i + by) % length) for i in range(length)])  129 us
    unnamed x1, blocking collectives  42 us
    dot_general x8, matrix products, attend_block(): jnp.einsum('qhd,khd->hqk', query_heads, key_heads, preferred_element_type...  15 us
    ppermute x32, starting transfers between devices, from_behind(): lax.ppermute(array, axis, [(i, (i + by) % length) for i in range(length)])  14.2 us
  transfers between devices with their start and end apart: 34, of which 16 were waited for; matrix products, arithmetic and copies ran while one was open for 2% of the time, Pallas kernels for 0%

commit v1 on v0

v1 whole, which is shorter than its diff:
```python
import functools
import math

import jax
import jax.numpy as jnp
from jax import lax
from jax.experimental import pallas as pl
from jax.experimental.pallas import tpu as pltpu
from jax.sharding import Mesh
from jax.sharding import PartitionSpec as P

HEADS = 16
HEAD_DIM = 128
SPAN = 32
DIGIT = 64
ROWS_PER_SPAN_PAIR = 2 * SPAN
EXTRA = 8
MASKED = -1e30
SCALE = 1.0 / math.sqrt(HEAD_DIM)
LOG2E = math.log2(math.e)
VMEM_LIMIT = 48 * 1024 * 1024


def pack_kernel(span_ref, half_ref, q_ref, k_ref, v_ref, out_ref):
    rows = q_ref.shape[0]
    for head in range(HEADS):
        lanes = slice(head * HEAD_DIM, (head + 1) * HEAD_DIM)
        out_ref[head, 0:rows, :] = q_ref[:, lanes]
        out_ref[head, rows : 2 * rows, :] = k_ref[:, lanes]
        out_ref[head, 2 * rows : 3 * rows, :] = v_ref[:, lanes]
    lane = lax.broadcasted_iota(jnp.int32, (EXTRA, HEAD_DIM), 1)
    row = lax.broadcasted_iota(jnp.int32, (EXTRA, HEAD_DIM), 0)
    local = lane - half_ref[0] * rows
    rank = jnp.where(local < SPAN, span_ref[0], span_ref[1])
    digit = jnp.where(row == 0, rank // DIGIT, rank % DIGIT)
    mine = (local >= 0) & (local < rows) & (row < 2)
    extra = jnp.where(mine, digit, 0).astype(jnp.float32).astype(jnp.bfloat16)
    for head in range(HEADS):
        out_ref[head, 3 * rows : 3 * rows + EXTRA, :] = extra


def positions(ref, rows):
    extra = ref[:, 3 * rows : 3 * rows + EXTRA, :].astype(jnp.float32)
    rank = extra[:, 0, :] * DIGIT + extra[:, 1, :]
    rank = jnp.sum(rank.reshape(HEADS // 2, 2, HEAD_DIM), axis=1)
    lane = lax.broadcasted_iota(jnp.int32, (HEADS // 2, HEAD_DIM), 1)
    return rank * SPAN + (lane % SPAN).astype(jnp.float32)


def step_kernel(first, last, *refs):
    if first:
        mine_ref, other_ref, *outs = refs
    else:
        mine_ref, other_ref, acc_in, stat_in, *outs = refs
    rows = (mine_ref.shape[1] - EXTRA) // 3
    total_rows = HEADS * rows
    query_pos = jnp.transpose(
        jnp.concatenate([positions(mine_ref, rows)] * (HEAD_DIM // (HEADS // 2)), axis=0)
    )
    key_pos = positions(other_ref, rows)
    keys = other_ref[:, rows : 2 * rows, :].reshape(total_rows, HEAD_DIM)
    values = other_ref[:, 2 * rows : 3 * rows, :].reshape(total_rows, HEAD_DIM)
    key_row = jnp.concatenate([key_pos[i : i + 1, :] for i in range(HEADS // 2)], axis=1)
    group = 4
    block = group * rows
    for index in range(HEADS // group):
        queries = mine_ref[index * group : (index + 1) * group, 0:rows, :].reshape(block, HEAD_DIM)
        scores = lax.dot_general(
            queries, keys, (((1,), (1,)), ((), ())), preferred_element_type=jnp.float32
        )
        per = block // HEAD_DIM
        query_col = jnp.concatenate(
            [query_pos[:, index * per + i : index * per + i + 1] for i in range(per)], axis=0
        )
        scores = jnp.where(key_row <= query_col, scores, MASKED)
        top = jnp.max(scores, axis=1, keepdims=True)
        here = slice(index * block, (index + 1) * block)
        if not first:
            old_top = stat_in[here, 0:1]
            top = jnp.maximum(top, old_top)
        weights = jnp.exp2((scores - top) * (SCALE * LOG2E))
        total = jnp.sum(weights, axis=1, keepdims=True)
        acc = jnp.dot(weights.astype(jnp.bfloat16), values, preferred_element_type=jnp.float32)
        if not first:
            factor = jnp.exp2((old_top - top) * (SCALE * LOG2E))
            total = total + stat_in[here, 1:2] * factor
            acc = acc + acc_in[here, :] * factor
        if last:
            out_ref = outs[0]
            result = (acc * (1.0 / total)).astype(jnp.bfloat16)
            out_ref[index * group : (index + 1) * group, 0:rows, :] = result.reshape(
                group, rows, HEAD_DIM
            )
            log_total = top * SCALE + jnp.log(total)
            for i in range(per):
                piece = jnp.broadcast_to(
                    log_total[i * HEAD_DIM : (i + 1) * HEAD_DIM], (HEAD_DIM, HEAD_DIM)
                )
                piece = jnp.transpose(piece)[0:EXTRA, :]
                high = piece.astype(jnp.bfloat16).astype(jnp.float32)
                rest = piece - high
                middle = rest.astype(jnp.bfloat16).astype(jnp.float32)
                low = rest - middle
                row = lax.broadcasted_iota(jnp.int32, piece.shape, 0)
                extra = jnp.where(row == 0, high, jnp.where(row == 1, middle, low))
                extra = extra.astype(jnp.bfloat16)
                for j in range(HEAD_DIM // rows):
                    out_ref[
                        index * group + i * (HEAD_DIM // rows) + j, rows : rows + EXTRA, :
                    ] = extra
        else:
            acc_out, stat_out = outs
            acc_out[here, :] = acc
            lane = lax.broadcasted_iota(jnp.int32, (block, HEAD_DIM), 1)
            stat_out[here, :] = jnp.where(lane == 0, top, total)


def unpack_kernel(half_ref, in_ref, out_ref, log_ref):
    rows = out_ref.shape[0]
    for head in range(HEADS):
        out_ref[:, head * HEAD_DIM : (head + 1) * HEAD_DIM] = in_ref[head, 0:rows, :]
    extra = in_ref[:, rows : rows + EXTRA, :].astype(jnp.float32)
    full = extra[:, 0, :] + extra[:, 1, :] + extra[:, 2, :]
    log_ref[...] = jnp.where(half_ref[0] == 0, full[:, 0:rows], full[:, rows : 2 * rows])


VMEM = pl.BlockSpec(memory_space=pltpu.VMEM)
SMEM = pl.BlockSpec(memory_space=pltpu.SMEM)


def call(kernel, out_shape, n_scalar, n_vector, flops=0, data=1 << 20):
    outs = out_shape if isinstance(out_shape, tuple) else None
    return pl.pallas_call(
        kernel,
        out_shape=out_shape,
        in_specs=[SMEM] * n_scalar + [VMEM] * n_vector,
        out_specs=tuple(VMEM for _ in outs) if outs else VMEM,
        compiler_params=pltpu.CompilerParams(vmem_limit_bytes=VMEM_LIMIT),
        cost_estimate=pl.CostEstimate(flops=flops, bytes_accessed=data, transcendentals=0),
    )


def local(queries, keys, values, span_order):
    rows = queries.shape[0]
    parts = lax.axis_size("part")
    half = (lax.axis_index("head") % 2).astype(jnp.int32).reshape(1)
    packed = call(
        pack_kernel,
        jax.ShapeDtypeStruct((HEADS, 3 * rows + EXTRA, HEAD_DIM), jnp.bfloat16),
        2,
        3,
    )(span_order, half, queries, keys, values)
    mine = lax.all_to_all(packed, "head", 0, 0, tiled=True)
    total_rows = HEADS * rows
    work = 4 * total_rows * total_rows * HEAD_DIM
    state = ()
    other = mine
    for part in range(parts):
        first, last = part == 0, part == parts - 1
        if last:
            shape = jax.ShapeDtypeStruct((HEADS, rows + EXTRA, HEAD_DIM), jnp.bfloat16)
        else:
            shape = (jax.ShapeDtypeStruct((total_rows, HEAD_DIM), jnp.float32),) * 2
        following = (
            None
            if last
            else lax.ppermute(other, "part", [(i, (i + 1) % parts) for i in range(parts)])
        )
        state = call(
            functools.partial(step_kernel, first, last), shape, 0, 2 if first else 4, work
        )(mine, other, *state)
        other = following
    back = lax.all_to_all(state, "head", 0, 0, tiled=True)
    return call(
        unpack_kernel,
        (
            jax.ShapeDtypeStruct((rows, HEADS * HEAD_DIM), jnp.bfloat16),
            jax.ShapeDtypeStruct((HEADS, rows), jnp.float32),
        ),
        1,
        1,
    )(half, back)


def solution(mesh):
    devices = mesh.devices.reshape(HEADS, -1)
    rows = P(("head", "part"), None)
    return jax.shard_map(
        local,
        mesh=Mesh(devices, ("head", "part")),
        in_specs=(rows, rows, rows, P(("head", "part"))),
        out_specs=(rows, P(None, ("head", "part"))),
        check_vma=False,
    )
```

time: 229 us -> 55.9 us (0.24)
  waiting for transfers between devices: 130 us -> 0.01 us
  matrix products: 18.7 us -> 0 us
  starting transfers between devices: 14.3 us -> 0.01 us
  between operations: 14.1 us -> 0.67 us
  Pallas kernels: 0 us -> 6.8 us
  other arithmetic: 5.65 us -> 0 us
  blocking collectives: 42 us -> 44.6 us
    ppermute x32 -> x1, waiting for transfers between devices: 129 us -> 0.01 us  [local(): lax.ppermute(other, 'part', [(i, (i + 1) % parts) for i in range(parts)])]
    all_to_all x0 -> x2, blocking collectives: none -> 44.6 us  [the longest x1 30 us: local(): mine = lax.all_to_all(packed, 'head', 0, 0, tiled=True)]
    unnamed x1 -> x0, blocking collectives: 42 us -> none
    dot_general x16 -> x0, matrix products: 18.7 us -> none  [the longest x8 15 us: attend_block(): jnp.einsum('qhd,khd->hqk', query_heads, key_heads, preferred_element_type...]
    ppermute x32 -> x1, starting transfers between devices: 14.2 us -> 0.01 us  [local(): lax.ppermute(other, 'part', [(i, (i + 1) % parts) for i in range(parts)])]
    pallas_call x0 -> x4, Pallas kernels: none -> 6.8 us  [the longest x2 5.34 us: local(): call(functools.partial(step_kernel, first, last), shape, 0, 2 if first el...]
    reduce_sum x8 -> x0, other arithmetic: 3.35 us -> none  [attend_block(): new_sum = run_sum * factor + jnp.sum(weights, axis=2)]
  transfers between devices with their start and end apart: 34 -> 1, of which waited for: 16 -> 0; matrix products, arithmetic and copies ran while one was open for 2% -> 0% of each run, Pallas kernels for 0% -> 4%
where the time goes in v1:
time: 55.9 us; the launch traced here: 55.6 us
  blocking collectives  44.6 us (80%)
  Pallas kernels  6.8 us (12%)
  local copies, waits for them, and re-layouts  3.5 us (6%)
  between operations  0.67 us (1%)
    all_to_all x1, blocking collectives, local(): mine = lax.all_to_all(packed, 'head', 0, 0, tiled=True)  30 us
    all_to_all x1, blocking collectives, local(): back = lax.all_to_all(state, 'head', 0, 0, tiled=True)  14.6 us
    pallas_call x2, Pallas kernels, local(): call(functools.partial(step_kernel, first, last), shape, 0, 2 if first el...  5.34 us
    unnamed x8, local copies, waits for them, and re-layouts  3.5 us
  transfers between devices with their start and end apart: 1, of which 0 were waited for; matrix products, arithmetic and copies ran while one was open for 0% of the time, Pallas kernels for 4%

profile of v1, /device:TPU:0, one launch (start us, length us, event | category | flops | bytes accessed | tf_op | source)
XLA Modules:
  0.0 55.6 jit_solution(17438712617533750286)
XLA Ops:
  0.6 0.0 copy-start.3
  0.7 0.6 %copy-done.3 = s32[2]{0:T(128)S(1)} copy-done((s32[2]{0:T(128)S(1)}, s32[2]{0:T(128)}, u32[]{:S(2)}) %copy-start.3) | copy-done | bytes 32
  1.3 0.0 copy-start
  1.3 0.9 %copy-done = bf16[64,2048]{1,0:T(8,128)(2,1)S(1)} copy-done((bf16[64,2048]{1,0:T(8,128)(2,1)S(1)}, bf16[64,2048]{1,0:T(8,128)(2,1)}, u32[]{:S(2)}) %copy-start) | copy-done | bytes 262168
  2.2 0.0 copy-start.1
  2.3 0.9 %copy-done.1 = bf16[64,2048]{1,0:T(8,128)(2,1)S(1)} copy-done((bf16[64,2048]{1,0:T(8,128)(2,1)S(1)}, bf16[64,2048]{1,0:T(8,128)(2,1)}, u32[]{:S(2)}) %copy-start.1) | copy-done | bytes 262168
  3.2 0.0 copy-start.2
  3.2 0.9 %copy-done.2 = bf16[64,2048]{1,0:T(8,128)(2,1)S(1)} copy-done((bf16[64,2048]{1,0:T(8,128)(2,1)S(1)}, bf16[64,2048]{1,0:T(8,128)(2,1)}, u32[]{:S(2)}) %copy-start.2) | copy-done | bytes 262168
  4.1 0.7 %shard_map.59 = bf16[16,200,128]{2,1,0:T(8,128)(2,1)S(1)} custom-call(s32[2]{0:T(128)S(1)} %copy-done.3, s32[1]{0:T(128)} %bitcast.half_ref, bf16[64,2048]{1,0:T(8,128)(2,1)S(1)} %copy-done, bf16[64,2048]{1,0:T(8,128)(2,1)S(1)} %copy-done.1, bf16[64,2048]{1,0:T(8,128)(2,1)S(1)} %copy-done.2), custom_call_target="tpu_custom_call" | custom-call | bytes 1048576 | tf_op jit(solution)/shard_map/pallas_call | solution.py:147
  4.8 30.0 %all_to_all.10.refs_0_.refs_1_ = bf16[16,200,128]{2,1,0:T(8,128)(2,1)S(1)} all-to-all(bf16[16,200,128]{2,1,0:T(8,128)(2,1)S(1)} %shard_map.59), channel_id=1, replica_groups=mesh['outer'=8,'inner'=4] {'outer','inner':(1)2}, dimensions={0} | all-to-all | bytes 1638400 | tf_op jit(solution)/shard_map/all_to_all | solution.py:153
  34.9 0.0 collective-permute-start
  34.9 2.3 %shard_map.60 = (f32[1024,128]{1,0:T(8,128)S(1)}, f32[1024,128]{1,0:T(8,128)S(1)}) custom-call(bf16[16,200,128]{2,1,0:T(8,128)(2,1)S(1)} %all_to_all.10.refs_0_.refs_1_, bf16[16,200,128]{2,1,0:T(8,128)(2,1)S(1)} %all_to_all.10.refs_0_.refs_1_), custom_call_target="tpu_custom_call" | custom-call | flops 536870912 | bytes 1048576 | tf_op jit(solution)/shard_map/pallas_call | solution.py:169
  37.2 0.0 collective-permute-done.refs_1_
  37.2 3.0 %shard_map.61 = bf16[16,72,128]{2,1,0:T(8,128)(2,1)S(1)} custom-call(bf16[16,200,128]{2,1,0:T(8,128)(2,1)S(1)} %all_to_all.10.refs_0_.refs_1_, bf16[16,200,128]{2,1,0:T(8,128)(2,1)S(1)} %collective-permute-done.refs_1_, f32[1024,128]{1,0:T(8,128)S(1)} %get-tuple-element.4.refs_2_, f32[1024,128]{1,0:T(8,128)S(1)} %get-tuple-element.5.refs_3_), custom_call_target="tpu_custom_call" | custom-call | flops 536870912 | bytes 1048576 | tf_op jit(solution)/shard_map/pallas_call | solution.py:169
  40.2 14.6 %all_to_all.11.in_ref = bf16[16,72,128]{2,1,0:T(8,128)(2,1)S(1)} all-to-all(bf16[16,72,128]{2,1,0:T(8,128)(2,1)S(1)} %shard_map.61), channel_id=1, replica_groups=mesh['outer'=8,'inner'=4] {'outer','inner':(1)2}, dimensions={0} | all-to-all | bytes 589824 | tf_op jit(solution)/shard_map/all_to_all | solution.py:173
  54.8 0.8 %shard_map.62 = (bf16[64,2048]{1,0:T(8,128)(2,1)}, f32[16,64]{1,0:T(8,128)}) custom-call(s32[1]{0:T(128)} %bitcast.half_ref, bf16[16,72,128]{2,1,0:T(8,128)(2,1)S(1)} %all_to_all.11.in_ref), custom_call_target="tpu_custom_call" | custom-call | bytes 1048576 | tf_op jit(solution)/shard_map/pallas_call | solution.py:174
Async XLA Ops:
  0.6 0.7 %copy-start.3 = (s32[2]{0:T(128)S(1)}, s32[2]{0:T(128)}, u32[]{:S(2)}) copy-start(s32[2]{0:T(128)} %span_ref.1) | copy-start | bytes 28
  1.3 0.9 %copy-start = (bf16[64,2048]{1,0:T(8,128)(2,1)S(1)}, bf16[64,2048]{1,0:T(8,128)(2,1)}, u32[]{:S(2)}) copy-start(bf16[64,2048]{1,0:T(8,128)(2,1)} %q_ref.1) | copy-start | bytes 786436
  2.2 0.9 %copy-start.1 = (bf16[64,2048]{1,0:T(8,128)(2,1)S(1)}, bf16[64,2048]{1,0:T(8,128)(2,1)}, u32[]{:S(2)}) copy-start(bf16[64,2048]{1,0:T(8,128)(2,1)} %k_ref.1) | copy-start | bytes 786436
  3.2 0.9 %copy-start.2 = (bf16[64,2048]{1,0:T(8,128)(2,1)S(1)}, bf16[64,2048]{1,0:T(8,128)(2,1)}, u32[]{:S(2)}) copy-start(bf16[64,2048]{1,0:T(8,128)(2,1)} %v_ref.1) | copy-start | bytes 786436
  34.9 2.3 %collective-permute-start = (bf16[16,200,128]{2,1,0:T(8,128)(2,1)S(1)}, bf16[16,200,128]{2,1,0:T(8,128)(2,1)S(1)}, u32[]{:S(2)}, u32[]{:S(2)}) collective-permute-start(bf16[16,200,128]{2,1,0:T(8,128)(2,1)S(1)} %all_to_all.10.refs_0_.refs_1_), channel_id=1, source_target_pairs={{0,1},{1,0},{2,3},{3,2},{4,5},{5,4},{6,7},{7,6},{8,9},{9,8},{10,11... | collective-permute-start | bytes 2457608 | tf_op jit(solution)/shard_map/ppermute | solution.py:167

commit v2 on v1

v2 whole, which is shorter than its diff:
```python
import functools
import math

import jax
import jax.numpy as jnp
from jax import lax
from jax.experimental import pallas as pl
from jax.experimental.pallas import tpu as pltpu
from jax.sharding import Mesh
from jax.sharding import PartitionSpec as P

HEADS = 16
HEAD_DIM = 128
SPAN = 32
DIGIT = 64
EXTRA = 8
GROUP = 4
MASKED = -1e30
SCALE = 1.0 / math.sqrt(HEAD_DIM)
SCALE2 = SCALE * math.log2(math.e)
VMEM_LIMIT = 48 * 1024 * 1024

VMEM = pl.BlockSpec(memory_space=pltpu.VMEM)
HBM = pl.BlockSpec(memory_space=pltpu.HBM)


def pack_kernel(span_hbm, q_hbm, k_hbm, v_hbm, out_ref, span, buffers, sems):
    rows = q_hbm.shape[0]
    span_copy = pltpu.make_async_copy(span_hbm, span, sems.at[3])
    span_copy.start()
    copies = [
        pltpu.make_async_copy(source, buffers.at[i], sems.at[i])
        for i, source in enumerate((q_hbm, k_hbm, v_hbm))
    ]
    for copy in copies:
        copy.start()
    span_copy.wait()
    lane = lax.broadcasted_iota(jnp.int32, (EXTRA, HEAD_DIM), 1)
    row = lax.broadcasted_iota(jnp.int32, (EXTRA, HEAD_DIM), 0)
    local = lane - (lax.axis_index("head") % 2) * rows
    rank = jnp.where(local < SPAN, span[0], span[1])
    digit = jnp.where(row == 0, rank // DIGIT, rank % DIGIT)
    mine = (local >= 0) & (local < rows) & (row < 2)
    extra = jnp.where(mine, digit, 0).astype(jnp.float32).astype(jnp.bfloat16)
    for head in range(HEADS):
        out_ref[head, 3 * rows : 3 * rows + EXTRA, :] = extra
    for i, copy in enumerate(copies):
        copy.wait()
        for head in range(HEADS):
            out_ref[head, i * rows : (i + 1) * rows, :] = buffers[
                i, :, head * HEAD_DIM : (head + 1) * HEAD_DIM
            ]


def positions(ref, rows):
    extra = ref[:, 3 * rows : 3 * rows + EXTRA, :].astype(jnp.float32)
    rank = extra[:, 0, :] * DIGIT + extra[:, 1, :]
    rank = jnp.sum(rank.reshape(HEADS // 2, 2, HEAD_DIM), axis=1)
    lane = lax.broadcasted_iota(jnp.int32, (HEADS // 2, HEAD_DIM), 1)
    return rank * SPAN + (lane % SPAN).astype(jnp.float32)


def attend_kernel(first, last, mine_ref, other_ref, *refs):
    if first:
        outs = refs
    else:
        acc_in, total_in, top_in, *outs = refs
    rows = (mine_ref.shape[1] - EXTRA) // 3
    keys_total = HEADS * rows
    block = GROUP * rows
    blocks = HEADS // GROUP
    tiles = block // HEAD_DIM
    keys = other_ref[:, rows : 2 * rows, :].reshape(keys_total, HEAD_DIM)

    def score(index):
        queries = mine_ref[index * GROUP : (index + 1) * GROUP, 0:rows, :]
        return lax.dot_general(
            queries.reshape(block, HEAD_DIM),
            keys,
            (((1,), (1,)), ((), ())),
            preferred_element_type=jnp.float32,
        )

    next_scores = score(0)
    repeat = HEAD_DIM // (HEADS // 2)
    query_pos = jnp.transpose(jnp.concatenate([positions(mine_ref, rows)] * repeat, axis=0))
    key_pos = positions(other_ref, rows)
    key_row = jnp.concatenate([key_pos[i : i + 1, :] for i in range(HEADS // 2)], axis=1)
    values = other_ref[:, 2 * rows : 3 * rows, :].reshape(keys_total, HEAD_DIM)
    values = jnp.concatenate([values, jnp.ones_like(values)], axis=1)
    lane = lax.broadcasted_iota(jnp.int32, (HEAD_DIM, HEAD_DIM), 1)
    all_top = jnp.zeros((HEAD_DIM, HEAD_DIM), jnp.float32)
    all_total = jnp.ones((HEAD_DIM, HEAD_DIM), jnp.float32)
    for index in range(blocks):
        scores = next_scores
        if index + 1 < blocks:
            next_scores = score(index + 1)
        query_col = jnp.concatenate(
            [query_pos[:, index * tiles + i : index * tiles + i + 1] for i in range(tiles)], axis=0
        )
        scores = jnp.where(key_row <= query_col, scores, MASKED)
        top = jnp.broadcast_to(jnp.max(scores, axis=1, keepdims=True), (block, HEAD_DIM))
        here = slice(index * block, (index + 1) * block)
        if not first:
            old_top = top_in[here, :]
            top = jnp.maximum(top, old_top)
            factor = jnp.exp2((old_top - top) * SCALE2)
        weights = jnp.exp2((scores - top[:, 0:1]) * SCALE2).astype(jnp.bfloat16)
        summed = jnp.dot(weights, values, preferred_element_type=jnp.float32)
        acc, total = summed[:, :HEAD_DIM], summed[:, HEAD_DIM:]
        if not first:
            acc = acc + acc_in[here, :] * factor
            total = total + total_in[here, :] * factor
        if last:
            result = (acc * (1.0 / total)).astype(jnp.bfloat16)
            outs[0][index * GROUP : (index + 1) * GROUP, 0:rows, :] = result.reshape(
                GROUP, rows, HEAD_DIM
            )
            for i in range(tiles):
                tile = slice(i * HEAD_DIM, (i + 1) * HEAD_DIM)
                all_top = jnp.where(lane == index * tiles + i, top[tile], all_top)
                all_total = jnp.where(lane == index * tiles + i, total[tile], all_total)
        else:
            outs[0][here, :] = acc
            outs[1][here, :] = total
            outs[2][here, :] = top
    if last:
        pairs = HEADS // 2
        log_total = jnp.transpose(all_top)[0:pairs] * SCALE
        log_total = log_total + jnp.log(jnp.transpose(all_total)[0:pairs])
        high = log_total.astype(jnp.bfloat16).astype(jnp.float32)
        middle = (log_total - high).astype(jnp.bfloat16).astype(jnp.float32)
        low = log_total - high - middle
        row = lax.broadcasted_iota(jnp.int32, (EXTRA, HEAD_DIM), 0)
        for pair in range(pairs):
            terms = [
                jnp.broadcast_to(term[pair : pair + 1, :], (EXTRA, HEAD_DIM))
                for term in (high, middle, low)
            ]
            extra = jnp.where(row == 0, terms[0], jnp.where(row == 1, terms[1], terms[2]))
            extra = extra.astype(jnp.bfloat16)
            for i in range(2):
                outs[0][2 * pair + i, rows : rows + EXTRA, :] = extra


def unpack_kernel(in_ref, out_ref, log_ref):
    rows = out_ref.shape[0]
    for head in range(HEADS):
        out_ref[:, head * HEAD_DIM : (head + 1) * HEAD_DIM] = in_ref[head, 0:rows, :]
    extra = in_ref[:, rows : rows + EXTRA, :].astype(jnp.float32)
    log_total = extra[:, 0, :] + extra[:, 1, :] + extra[:, 2, :]
    half = lax.axis_index("head") % 2
    log_ref[...] = jnp.where(half == 0, log_total[:, 0:rows], log_total[:, rows : 2 * rows])


def params():
    return pltpu.CompilerParams(vmem_limit_bytes=VMEM_LIMIT)


def local(queries, keys, values, span_order):
    rows = queries.shape[0]
    parts = lax.axis_size("part")
    in_hbm = [
        pltpu.with_memory_space_constraint(array, pltpu.HBM)
        for array in (span_order, queries, keys, values)
    ]
    packed = pl.pallas_call(
        pack_kernel,
        out_shape=jax.ShapeDtypeStruct((HEADS, 3 * rows + EXTRA, HEAD_DIM), jnp.bfloat16),
        in_specs=[HBM] * 4,
        out_specs=VMEM,
        scratch_shapes=[
            pltpu.SMEM(span_order.shape, jnp.int32),
            pltpu.VMEM((3,) + queries.shape, jnp.bfloat16),
            pltpu.SemaphoreType.DMA((4,)),
        ],
        compiler_params=params(),
    )(*in_hbm)
    mine = lax.all_to_all(packed, "head", 0, 0, tiled=True)
    total_rows = HEADS * rows
    ring = [(i, (i + 1) % parts) for i in range(parts)]
    state = ()
    other = mine
    for part in range(parts):
        first, last = part == 0, part == parts - 1
        if last:
            shapes = (jax.ShapeDtypeStruct((HEADS, rows + EXTRA, HEAD_DIM), jnp.bfloat16),)
            following = None
        else:
            shapes = (jax.ShapeDtypeStruct((total_rows, HEAD_DIM), jnp.float32),) * 3
            following = lax.ppermute(other, "part", ring)
        state = pl.pallas_call(
            functools.partial(attend_kernel, first, last),
            out_shape=shapes,
            in_specs=[VMEM] * (2 + len(state)),
            out_specs=(VMEM,) * len(shapes),
            compiler_params=params(),
            cost_estimate=pl.CostEstimate(
                flops=4 * total_rows * total_rows * HEAD_DIM,
                bytes_accessed=1 << 20,
                transcendentals=total_rows * total_rows,
            ),
        )(mine, other, *state)
        other = following
    back = lax.all_to_all(state[0], "head", 0, 0, tiled=True)
    return pl.pallas_call(
        unpack_kernel,
        out_shape=(
            jax.ShapeDtypeStruct((rows, HEADS * HEAD_DIM), jnp.bfloat16),
            jax.ShapeDtypeStruct((HEADS, rows), jnp.float32),
        ),
        in_specs=[VMEM],
        out_specs=(VMEM, VMEM),
        compiler_params=params(),
    )(back)


def solution(mesh):
    rows = P(("head", "part"), None)
    return jax.shard_map(
        local,
        mesh=Mesh(mesh.devices.reshape(HEADS, -1), ("head", "part")),
        in_specs=(rows, rows, rows, P(("head", "part"))),
        out_specs=(rows, P(None, ("head", "part"))),
        check_vma=False,
    )
```

time: 55.9 us -> 51.4 us (0.919)
  local copies, waits for them, and re-layouts: 3.5 us -> 0 us
  Pallas kernels: 6.8 us -> 5.57 us
  waiting for transfers between devices: 0.01 us -> 0.73 us
    unnamed x8 -> x0, local copies, waits for them, and re-layouts: 3.5 us -> none
    pallas_call x4, Pallas kernels: 6.8 us -> 5.57 us  [the longest x2 3.62 us: local(): pl.pallas_call(functools.partial(attend_kernel, first, last), out_shape=s...]
    ppermute x1, waiting for transfers between devices: 0.01 us -> 0.73 us  [local(): following = lax.ppermute(other, 'part', ring)]
  transfers between devices with their start and end apart: 1 -> 1, of which waited for: 0 -> 1; matrix products, arithmetic and copies ran while one was open for 0% -> 0% of each run, Pallas kernels for 4% -> 3%
where the time goes in v2:
time: 51.4 us; the launch traced here: 51.2 us
  blocking collectives  44.2 us (86%)
  Pallas kernels  5.57 us (11%)
  waiting for transfers between devices  0.73 us (1%)
  between operations  0.66 us (1%)
    all_to_all x1, blocking collectives, local(): mine = lax.all_to_all(packed, 'head', 0, 0, tiled=True)  30 us
    all_to_all x1, blocking collectives, local(): back = lax.all_to_all(state[0], 'head', 0, 0, tiled=True)  14.2 us
    pallas_call x2, Pallas kernels, local(): pl.pallas_call(functools.partial(attend_kernel, first, last), out_shape=s...  3.62 us
    pallas_call x1, Pallas kernels, local(): pl.pallas_call(pack_kernel, out_shape=jax.ShapeDtypeStruct((HEADS, 3 * ro...  1.19 us
  transfers between devices with their start and end apart: 1, of which 1 were waited for; matrix products, arithmetic and copies ran while one was open for 0% of the time, Pallas kernels for 3%

profile of v2, /device:TPU:0, one launch (start us, length us, event | category | flops | bytes accessed | tf_op | source)
XLA Modules:
  0.0 51.2 jit_solution(6644327580923726368)
XLA Ops:
  0.6 1.2 %shard_map.59 = bf16[16,200,128]{2,1,0:T(8,128)(2,1)S(1)} custom-call(s32[2]{0:T(128)} %span_hbm.1, bf16[64,2048]{1,0:T(8,128)(2,1)} %q_hbm.1, bf16[64,2048]{1,0:T(8,128)(2,1)} %k_hbm.1, bf16[64,2048]{1,0:T(8,128)(2,1)} %v_hbm.1), custom_call_target="tpu_custom_call" | custom-call | tf_op jit(solution)/shard_map/pallas_call | solution.py:167
  1.8 30.0 %all_to_all.10.mine_ref.other_ref = bf16[16,200,128]{2,1,0:T(8,128)(2,1)S(1)} all-to-all(bf16[16,200,128]{2,1,0:T(8,128)(2,1)S(1)} %shard_map.59), channel_id=1, replica_groups=mesh['outer'=8,'inner'=4] {'outer','inner':(1)2}, dimensions={0} | all-to-all | bytes 1638400 | tf_op jit(solution)/shard_map/all_to_all | solution.py:179
  31.9 0.0 collective-permute-start
  31.9 1.6 %shard_map.60 = (f32[1024,128]{1,0:T(8,128)S(1)}, f32[1024,128]{1,0:T(8,128)S(1)}, f32[1024,128]{1,0:T(8,128)S(1)}) custom-call(bf16[16,200,128]{2,1,0:T(8,128)(2,1)S(1)} %all_to_all.10.mine_ref.other_ref, bf16[16,200,128]{2,1,0:T(8,128)(2,1)S(1)} %all_to_all.10.mine_ref.other_ref), custom_call_target="tpu_custom_call" | custom-call | flops 536870912 | bytes 1048576 | tf_op jit(solution)/shard_map/pallas_call | solution.py:192
  33.5 0.7 %collective-permute-done.other_ref = bf16[16,200,128]{2,1,0:T(8,128)(2,1)S(1)} collective-permute-done((bf16[16,200,128]{2,1,0:T(8,128)(2,1)S(1)}, bf16[16,200,128]{2,1,0:T(8,128)(2,1)S(1)}, u32[]{:S(2)}, u32[]{:S(2)}) %collective-permute-start) | collective-permute-done | bytes 819232 | tf_op jit(solution)/shard_map/ppermute | solution.py:191
  34.2 2.0 %shard_map.61 = bf16[16,72,128]{2,1,0:T(8,128)(2,1)S(1)} custom-call(bf16[16,200,128]{2,1,0:T(8,128)(2,1)S(1)} %all_to_all.10.mine_ref.other_ref, bf16[16,200,128]{2,1,0:T(8,128)(2,1)S(1)} %collective-permute-done.other_ref, f32[1024,128]{1,0:T(8,128)S(1)} %get-tuple-element.5.refs_0_, f32[1024,128]{1,0:T(8,128)S(1)} %get-tuple-element.6.refs_1_, ...), custom_call_target="tpu_custom_call" | custom-call | flops 536870912 | bytes 1048576 | tf_op jit(solution)/shard_map/pallas_call | solution.py:192
  36.2 14.2 %all_to_all.11.in_ref = bf16[16,72,128]{2,1,0:T(8,128)(2,1)S(1)} all-to-all(bf16[16,72,128]{2,1,0:T(8,128)(2,1)S(1)} %shard_map.61), channel_id=1, replica_groups=mesh['outer'=8,'inner'=4] {'outer','inner':(1)2}, dimensions={0} | all-to-all | bytes 589824 | tf_op jit(solution)/shard_map/all_to_all | solution.py:205
  50.4 0.8 %shard_map.62 = (bf16[64,2048]{1,0:T(8,128)(2,1)}, f32[16,64]{1,0:T(8,128)}) custom-call(bf16[16,72,128]{2,1,0:T(8,128)(2,1)S(1)} %all_to_all.11.in_ref), custom_call_target="tpu_custom_call" | custom-call | tf_op jit(solution)/shard_map/pallas_call | solution.py:206
Async XLA Ops:
  31.9 2.3 %collective-permute-start = (bf16[16,200,128]{2,1,0:T(8,128)(2,1)S(1)}, bf16[16,200,128]{2,1,0:T(8,128)(2,1)S(1)}, u32[]{:S(2)}, u32[]{:S(2)}) collective-permute-start(bf16[16,200,128]{2,1,0:T(8,128)(2,1)S(1)} %all_to_all.10.mine_ref.other_ref), channel_id=1, source_target_pairs={{0,1},{1,0},{2,3},{3,2},{4,5},{5,4},{6,7},{7,6},{8,9},{9,8},{10,11... | collective-permute-start | bytes 2457608 | tf_op jit(solution)/shard_map/ppermute | solution.py:191

commit v3 on v2

v3 whole, which is shorter than its diff:
```python
import functools
import math

import jax
import jax.numpy as jnp
from jax import lax
from jax.experimental import pallas as pl
from jax.experimental.pallas import tpu as pltpu
from jax.sharding import Mesh
from jax.sharding import PartitionSpec as P

HEADS = 16
HEAD_DIM = 128
SPAN = 32
DIGIT = 64
SPANS = 2
SOURCES = HEADS * SPANS
QUARTERS = HEAD_DIM // SPAN
EXTRA = 2
GROUP = 8
MASKED = -1e30
SCALE = 1.0 / math.sqrt(HEAD_DIM)
SCALE2 = SCALE * math.log2(math.e)
VMEM_LIMIT = 48 * 1024 * 1024

VMEM = pl.BlockSpec(memory_space=pltpu.VMEM)
HBM = pl.BlockSpec(memory_space=pltpu.HBM)


def flat(ref):
    count, half, two, lanes = ref.shape
    return ref.reshape(count, half * two, lanes)


def messages(rows):
    return jax.ShapeDtypeStruct((SOURCES, (rows + EXTRA) // 2, 2, HEAD_DIM), jnp.bfloat16)


def quarter(exchange):
    return lax.axis_index(exchange) % QUARTERS


def pack_kernel(exchange, span_hbm, q_hbm, k_hbm, v_hbm, out_ref, ranks, buffers, sems):
    span_copy = pltpu.make_async_copy(span_hbm, ranks, sems.at[3])
    span_copy.start()
    copies = [
        pltpu.make_async_copy(source, buffers.at[i], sems.at[i])
        for i, source in enumerate((q_hbm, k_hbm, v_hbm))
    ]
    for copy in copies:
        copy.start()
    out = flat(out_ref)
    span_copy.wait()
    lane = lax.broadcasted_iota(jnp.int32, (EXTRA, HEAD_DIM), 1)
    row = lax.broadcasted_iota(jnp.int32, (EXTRA, HEAD_DIM), 0)
    for span in range(SPANS):
        digit = jnp.where(row == 0, ranks[span] // DIGIT, ranks[span] % DIGIT)
        extra = jnp.where(lane // SPAN == quarter(exchange), digit, 0)
        extra = extra.astype(jnp.float32).astype(jnp.bfloat16)
        for head in range(HEADS):
            out[SPANS * head + span, 3 * SPAN : 3 * SPAN + EXTRA, :] = extra
    for i, copy in enumerate(copies):
        copy.wait()
        for head in range(HEADS):
            for span in range(SPANS):
                out[SPANS * head + span, i * SPAN : (i + 1) * SPAN, :] = buffers[
                    i, span * SPAN : (span + 1) * SPAN, head * HEAD_DIM : (head + 1) * HEAD_DIM
                ]


def positions(ref):
    extra = flat(ref)[:, 3 * SPAN : 3 * SPAN + EXTRA, :].astype(jnp.float32)
    rank = extra[:, 0, :] * DIGIT + extra[:, 1, :]
    rank = jnp.sum(rank.reshape(SOURCES // QUARTERS, QUARTERS, HEAD_DIM), axis=1)
    lane = lax.broadcasted_iota(jnp.int32, rank.shape, 1)
    return rank * SPAN + (lane % SPAN).astype(jnp.float32)


def attend_kernel(first, last, mine_ref, other_ref, *refs):
    if first:
        outs = refs
    else:
        acc_in, total_in, top_in, *outs = refs
    mine, other = flat(mine_ref), flat(other_ref)
    block = GROUP * SPAN
    blocks = SOURCES // GROUP
    tiles = block // HEAD_DIM
    groups = SOURCES // QUARTERS
    keys = other[:, SPAN : 2 * SPAN, :].reshape(SOURCES * SPAN, HEAD_DIM)

    def score(index):
        queries = mine[index * GROUP : (index + 1) * GROUP, 0:SPAN, :]
        return lax.dot_general(
            queries.reshape(block, HEAD_DIM),
            keys,
            (((1,), (1,)), ((), ())),
            preferred_element_type=jnp.float32,
        )

    next_scores = score(0)
    query_pos = jnp.concatenate([positions(mine_ref)] * (HEAD_DIM // groups), axis=0)
    query_pos = jnp.transpose(query_pos)
    key_pos = positions(other_ref)
    key_row = jnp.concatenate([key_pos[i : i + 1, :] for i in range(groups)], axis=1)
    values = other[:, 2 * SPAN : 3 * SPAN, :].reshape(SOURCES * SPAN, HEAD_DIM)
    values = jnp.concatenate([values, jnp.ones_like(values)], axis=1)
    lane = lax.broadcasted_iota(jnp.int32, (HEAD_DIM, HEAD_DIM), 1)
    all_top = jnp.zeros((HEAD_DIM, HEAD_DIM), jnp.float32)
    all_total = jnp.ones((HEAD_DIM, HEAD_DIM), jnp.float32)
    for index in range(blocks):
        scores = next_scores
        if index + 1 < blocks:
            next_scores = score(index + 1)
        query_col = jnp.concatenate(
            [query_pos[:, index * tiles + i : index * tiles + i + 1] for i in range(tiles)], axis=0
        )
        scores = jnp.where(key_row <= query_col, scores, MASKED)
        top = jnp.broadcast_to(jnp.max(scores, axis=1, keepdims=True), (block, HEAD_DIM))
        here = slice(index * block, (index + 1) * block)
        if not first:
            old_top = top_in[here, :]
            top = jnp.maximum(top, old_top)
            factor = jnp.exp2((old_top - top) * SCALE2)
        weights = jnp.exp2((scores - top[:, 0:1]) * SCALE2).astype(jnp.bfloat16)
        summed = jnp.dot(weights, values, preferred_element_type=jnp.float32)
        acc, total = summed[:, :HEAD_DIM], summed[:, HEAD_DIM:]
        if not first:
            acc = acc + acc_in[here, :] * factor
            total = total + total_in[here, :] * factor
        if last:
            result = (acc * (1.0 / total)).astype(jnp.bfloat16)
            flat(outs[0])[index * GROUP : (index + 1) * GROUP, 0:SPAN, :] = result.reshape(
                GROUP, SPAN, HEAD_DIM
            )
            for i in range(tiles):
                tile = slice(i * HEAD_DIM, (i + 1) * HEAD_DIM)
                all_top = jnp.where(lane == index * tiles + i, top[tile], all_top)
                all_total = jnp.where(lane == index * tiles + i, total[tile], all_total)
        else:
            outs[0][here, :] = acc
            outs[1][here, :] = total
            outs[2][here, :] = top
    if last:
        log_total = jnp.transpose(all_top)[0:groups] * SCALE
        log_total = log_total + jnp.log(jnp.transpose(all_total)[0:groups])
        high = log_total.astype(jnp.bfloat16).astype(jnp.float32)
        low = log_total - high
        row = lax.broadcasted_iota(jnp.int32, (EXTRA, HEAD_DIM), 0)
        for i in range(groups):
            extra = jnp.where(row == 0, high[i : i + 1, :], low[i : i + 1, :])
            extra = extra.astype(jnp.bfloat16)
            for j in range(QUARTERS):
                flat(outs[0])[QUARTERS * i + j, SPAN : SPAN + EXTRA, :] = extra


def unpack_kernel(exchange, in_ref, out_ref, log_ref):
    back = flat(in_ref)
    for head in range(HEADS):
        for span in range(SPANS):
            out_ref[
                span * SPAN : (span + 1) * SPAN, head * HEAD_DIM : (head + 1) * HEAD_DIM
            ] = back[SPANS * head + span, 0:SPAN, :]
    extra = back[:, SPAN : SPAN + EXTRA, :].astype(jnp.float32)
    log_total = (extra[:, 0, :] + extra[:, 1, :]).reshape(HEADS, SPANS, HEAD_DIM)
    mine = log_total[:, :, 0:SPAN]
    for i in range(1, QUARTERS):
        mine = jnp.where(quarter(exchange) == i, log_total[:, :, i * SPAN : (i + 1) * SPAN], mine)
    for span in range(SPANS):
        log_ref[:, span * SPAN : (span + 1) * SPAN] = mine[:, span, :]


def params():
    return pltpu.CompilerParams(vmem_limit_bytes=VMEM_LIMIT)


def local(everywhere, exchange, queries, keys, values, span_order):
    rows = queries.shape[0]
    devices = lax.axis_size(everywhere)
    parts = devices // HEADS
    in_hbm = [
        pltpu.with_memory_space_constraint(array, pltpu.HBM)
        for array in (span_order, queries, keys, values)
    ]
    packed = pl.pallas_call(
        functools.partial(pack_kernel, exchange),
        out_shape=messages(3 * SPAN),
        in_specs=[HBM] * 4,
        out_specs=VMEM,
        scratch_shapes=[
            pltpu.SMEM(span_order.shape, jnp.int32),
            pltpu.VMEM((3,) + queries.shape, jnp.bfloat16),
            pltpu.SemaphoreType.DMA((4,)),
        ],
        compiler_params=params(),
    )(*in_hbm)
    mine = lax.all_to_all(packed, exchange, 0, 0, tiled=True)
    total_rows = SOURCES * SPAN
    ring = [(i, i // parts * parts + (i + 1) % parts) for i in range(devices)]
    state = ()
    other = mine
    for part in range(parts):
        first, last = part == 0, part == parts - 1
        if last:
            shapes = (messages(SPAN),)
            following = None
        else:
            shapes = (jax.ShapeDtypeStruct((total_rows, HEAD_DIM), jnp.float32),) * 3
            following = lax.ppermute(other, everywhere, ring)
        state = pl.pallas_call(
            functools.partial(attend_kernel, first, last),
            out_shape=shapes,
            in_specs=[VMEM] * (2 + len(state)),
            out_specs=(VMEM,) * len(shapes),
            compiler_params=params(),
            cost_estimate=pl.CostEstimate(
                flops=4 * total_rows * total_rows * HEAD_DIM,
                bytes_accessed=1 << 20,
                transcendentals=total_rows * total_rows,
            ),
        )(mine, other, *state)
        other = following
    back = lax.all_to_all(state[0], exchange, 0, 0, tiled=True)
    return pl.pallas_call(
        functools.partial(unpack_kernel, exchange),
        out_shape=(
            jax.ShapeDtypeStruct((rows, HEADS * HEAD_DIM), jnp.bfloat16),
            jax.ShapeDtypeStruct((HEADS, rows), jnp.float32),
        ),
        in_specs=[VMEM],
        out_specs=(VMEM, VMEM),
        compiler_params=params(),
    )(back)


def solution(mesh):
    devices = mesh.devices.reshape(HEADS, -1, SPANS)
    if devices.shape[1] == 1:
        devices, everywhere, exchange = devices.reshape(-1), ("source",), ("source",)
    else:
        everywhere, exchange = ("head", "ring", "core"), ("head", "core")
    rows = P(everywhere, None)
    return jax.shard_map(
        functools.partial(local, everywhere, exchange),
        mesh=Mesh(devices, everywhere),
        in_specs=(rows, rows, rows, P(everywhere)),
        out_specs=(rows, P(None, everywhere)),
        check_vma=False,
    )
```

time: 51.4 us -> 50.7 us (0.986)
  blocking collectives: 44.2 us -> 42.6 us
  Pallas kernels: 5.57 us -> 6.87 us
    all_to_all x2, blocking collectives: 44.2 us -> 42.6 us  [the longest x1 28.1 us: local(): mine = lax.all_to_all(packed, exchange, 0, 0, tiled=True)]
    pallas_call x2, Pallas kernels: 1.95 us -> 2.68 us  [the longest x1 1.6 us: local(): pl.pallas_call(functools.partial(pack_kernel, exchange), out_shape=messag...]
    pallas_call x2, Pallas kernels: 3.62 us -> 4.19 us  [local(): pl.pallas_call(functools.partial(attend_kernel, first, last), out_shape=s...]
  transfers between devices with their start and end apart: 1 -> 1, of which waited for: 1 -> 1; matrix products, arithmetic and copies ran while one was open for 0% -> 0% of each run, Pallas kernels for 3% -> 4%
where the time goes in v3:
time: 50.7 us; the launch traced here: 50.6 us
  blocking collectives  42.6 us (84%)
  Pallas kernels  6.87 us (14%)
  between operations  0.66 us (1%)
    all_to_all x1, blocking collectives, local(): mine = lax.all_to_all(packed, exchange, 0, 0, tiled=True)  28.1 us
    all_to_all x1, blocking collectives, local(): back = lax.all_to_all(state[0], exchange, 0, 0, tiled=True)  14.5 us
    pallas_call x2, Pallas kernels, local(): pl.pallas_call(functools.partial(attend_kernel, first, last), out_shape=s...  4.19 us
    pallas_call x1, Pallas kernels, local(): pl.pallas_call(functools.partial(pack_kernel, exchange), out_shape=messag...  1.6 us
    pallas_call x1, Pallas kernels, local(): pl.pallas_call(functools.partial(unpack_kernel, exchange), out_shape=(jax...  1.08 us
  transfers between devices with their start and end apart: 1, of which 1 were waited for; matrix products, arithmetic and copies ran while one was open for 0% of the time, Pallas kernels for 4%

profile of v3, /device:TPU:0, one launch (start us, length us, event | category | flops | bytes accessed | tf_op | source)
XLA Modules:
  0.0 50.6 jit_solution(1702651829240470828)
XLA Ops:
  0.6 1.6 %shard_map.59 = bf16[32,49,2,128]{3,2,1,0:T(2,128)(2,1)S(1)} custom-call(s32[2]{0:T(128)} %span_hbm.1, bf16[64,2048]{1,0:T(8,128)(2,1)} %q_hbm.1, bf16[64,2048]{1,0:T(8,128)(2,1)} %k_hbm.1, bf16[64,2048]{1,0:T(8,128)(2,1)} %v_hbm.1), custom_call_target="tpu_custom_call" | custom-call | tf_op jit(solution)/shard_map/pallas_call | solution.py:184
  2.2 28.1 %all_to_all.10.mine_ref.other_ref = bf16[32,49,2,128]{3,2,1,0:T(2,128)(2,1)S(1)} all-to-all(bf16[32,49,2,128]{3,2,1,0:T(2,128)(2,1)S(1)} %shard_map.59), channel_id=1, replica_groups=mesh['outer'=8,'inner'=4] {'outer','inner'}, dimensions={0} | all-to-all | bytes 1605632 | tf_op jit(solution)/shard_map/all_to_all | solution.py:196
  30.3 0.0 collective-permute-start
  30.3 1.9 %shard_map.60 = (f32[1024,128]{1,0:T(8,128)S(1)}, f32[1024,128]{1,0:T(8,128)S(1)}, f32[1024,128]{1,0:T(8,128)S(1)}) custom-call(bf16[32,49,2,128]{3,2,1,0:T(2,128)(2,1)S(1)} %all_to_all.10.mine_ref.other_ref, bf16[32,49,2,128]{3,2,1,0:T(2,128)(2,1)S(1)} %all_to_all.10.mine_ref.other_ref), custom_call_target="tpu_custom_call" | custom-call | flops 536870912 | bytes 1048576 | tf_op jit(solution)/shard_map/pallas_call | solution.py:209
  32.2 0.4 collective-permute-done.other_ref
  32.6 2.3 %shard_map.61 = bf16[32,17,2,128]{3,2,1,0:T(2,128)(2,1)S(1)} custom-call(bf16[32,49,2,128]{3,2,1,0:T(2,128)(2,1)S(1)} %all_to_all.10.mine_ref.other_ref, bf16[32,49,2,128]{3,2,1,0:T(2,128)(2,1)S(1)} %collective-permute-done.other_ref, f32[1024,128]{1,0:T(8,128)S(1)} %get-tuple-element.5.refs_0_, f32[1024,128]{1,0:T(8,128)S(1)} %get-tuple-element.6.refs_1_, ...), custom_call_target="tpu_custom_call" | custom-call | flops 536870912 | bytes 1048576 | tf_op jit(solution)/shard_map/pallas_call | solution.py:209
  35.0 14.5 %all_to_all.11.in_ref = bf16[32,17,2,128]{3,2,1,0:T(2,128)(2,1)S(1)} all-to-all(bf16[32,17,2,128]{3,2,1,0:T(2,128)(2,1)S(1)} %shard_map.61), channel_id=1, replica_groups=mesh['outer'=8,'inner'=4] {'outer','inner'}, dimensions={0} | all-to-all | bytes 557056 | tf_op jit(solution)/shard_map/all_to_all | solution.py:222
  49.5 1.1 %shard_map.62 = (bf16[64,2048]{1,0:T(8,128)(2,1)}, f32[16,64]{1,0:T(8,128)}) custom-call(bf16[32,17,2,128]{3,2,1,0:T(2,128)(2,1)S(1)} %all_to_all.11.in_ref), custom_call_target="tpu_custom_call" | custom-call | tf_op jit(solution)/shard_map/pallas_call | solution.py:223
Async XLA Ops:
  30.3 2.3 %collective-permute-start = (bf16[32,49,2,128]{3,2,1,0:T(2,128)(2,1)S(1)}, bf16[32,49,2,128]{3,2,1,0:T(2,128)(2,1)S(1)}, u32[]{:S(2)}, u32[]{:S(2)}) collective-permute-start(bf16[32,49,2,128]{3,2,1,0:T(2,128)(2,1)S(1)} %all_to_all.10.mine_ref.other_ref), channel_id=1, source_target_pairs={{0,1},{1,0},{2,3},{3,2},{4,5},{5,4},{6,7},{7,6},{8,9},{9,8},{10,11... | collective-permute-start | bytes 2408456 | tf_op jit(solution)/shard_map/ppermute | solution.py:208

commit v4 on v3

--- a/solution.py
+++ b/solution.py
@@ -17,6 +17,8 @@
 SOURCES = HEADS * SPANS
 QUARTERS = HEAD_DIM // SPAN
 EXTRA = 2
+THERE = 3 * SPAN + EXTRA
+BACK = SPAN + EXTRA
 GROUP = 8
 MASKED = -1e30
 SCALE = 1.0 / math.sqrt(HEAD_DIM)
@@ -27,13 +29,17 @@
 HBM = pl.BlockSpec(memory_space=pltpu.HBM)
 
 
-def flat(ref):
-    count, half, two, lanes = ref.shape
-    return ref.reshape(count, half * two, lanes)
-
-
-def messages(rows):
-    return jax.ShapeDtypeStruct((SOURCES, (rows + EXTRA) // 2, 2, HEAD_DIM), jnp.bfloat16)
+def rows_of(message, size, first, count):
+    return slice(message * size + first, message * size + first + count)
+
+
+def messages(size):
+    return jax.ShapeDtypeStruct((SOURCES * size, HEAD_DIM), jnp.bfloat16)
+
+
+def exchanged(array, exchange):
+    paired = array.reshape(SOURCES, -1, 2, HEAD_DIM)
+    return lax.all_to_all(paired, exchange, 0, 0, tiled=True).reshape(array.shape)
 
 
 def quarter(exchange):
@@ -49,7 +55,6 @@
     ]
     for copy in copies:
         copy.start()
-    out = flat(out_ref)
     span_copy.wait()
     lane = lax.broadcasted_iota(jnp.int32, (EXTRA, HEAD_DIM), 1)
     row = lax.broadcasted_iota(jnp.int32, (EXTRA, HEAD_DIM), 0)
@@ -58,22 +63,31 @@
         extra = jnp.where(lane // SPAN == quarter(exchange), digit, 0)
         extra = extra.astype(jnp.float32).astype(jnp.bfloat16)
         for head in range(HEADS):
-            out[SPANS * head + span, 3 * SPAN : 3 * SPAN + EXTRA, :] = extra
+            out_ref[rows_of(SPANS * head + span, THERE, 3 * SPAN, EXTRA), :] = extra
     for i, copy in enumerate(copies):
         copy.wait()
         for head in range(HEADS):
             for span in range(SPANS):
-                out[SPANS * head + span, i * SPAN : (i + 1) * SPAN, :] = buffers[
+                out_ref[rows_of(SPANS * head + span, THERE, i * SPAN, SPAN), :] = buffers[
                     i, span * SPAN : (span + 1) * SPAN, head * HEAD_DIM : (head + 1) * HEAD_DIM
                 ]
 
 
 def positions(ref):
-    extra = flat(ref)[:, 3 * SPAN : 3 * SPAN + EXTRA, :].astype(jnp.float32)
-    rank = extra[:, 0, :] * DIGIT + extra[:, 1, :]
-    rank = jnp.sum(rank.reshape(SOURCES // QUARTERS, QUARTERS, HEAD_DIM), axis=1)
+    ranks = []
+    for i in range(0, SOURCES, QUARTERS):
+        extras = [ref[rows_of(i + j, THERE, 3 * SPAN, EXTRA), :] for j in range(QUARTERS)]
+        digits = sum(extra.astype(jnp.float32) for extra in extras)
+        ranks.append(digits[0:1] * DIGIT + digits[1:2])
+    rank = jnp.concatenate(ranks, axis=0)
     lane = lax.broadcasted_iota(jnp.int32, rank.shape, 1)
     return rank * SPAN + (lane % SPAN).astype(jnp.float32)
+
+
+def spans(ref, sources, which):
+    return jnp.concatenate(
+        [ref[rows_of(source, THERE, which * SPAN, SPAN), :] for source in sources], axis=0
+    )
 
 
 def attend_kernel(first, last, mine_ref, other_ref, *refs):
@@ -81,17 +95,15 @@
         outs = refs
     else:
         acc_in, total_in, top_in, *outs = refs
-    mine, other = flat(mine_ref), flat(other_ref)
     block = GROUP * SPAN
     blocks = SOURCES // GROUP
     tiles = block // HEAD_DIM
     groups = SOURCES // QUARTERS
-    keys = other[:, SPAN : 2 * SPAN, :].reshape(SOURCES * SPAN, HEAD_DIM)
+    keys = spans(other_ref, range(SOURCES), 1)
 
     def score(index):
-        queries = mine[index * GROUP : (index + 1) * GROUP, 0:SPAN, :]
         return lax.dot_general(
-            queries.reshape(block, HEAD_DIM),
+            spans(mine_ref, range(index * GROUP, (index + 1) * GROUP), 0),
             keys,
             (((1,), (1,)), ((), ())),
             preferred_element_type=jnp.float32,
@@ -102,7 +114,7 @@
     query_pos = jnp.transpose(query_pos)
     key_pos = positions(other_ref)
     key_row = jnp.concatenate([key_pos[i : i + 1, :] for i in range(groups)], axis=1)
-    values = other[:, 2 * SPAN : 3 * SPAN, :].reshape(SOURCES * SPAN, HEAD_DIM)
+    values = spans(other_ref, range(SOURCES), 2)
     values = jnp.concatenate([values, jnp.ones_like(values)], axis=1)
     lane = lax.broadcasted_iota(jnp.int32, (HEAD_DIM, HEAD_DIM), 1)
     all_top = jnp.zeros((HEAD_DIM, HEAD_DIM), jnp.float32)
@@ -129,9 +141,9 @@
             total = total + total_in[here, :] * factor
         if last:
             result = (acc * (1.0 / total)).astype(jnp.bfloat16)
-            flat(outs[0])[index * GROUP : (index + 1) * GROUP, 0:SPAN, :] = result.reshape(
-                GROUP, SPAN, HEAD_DIM
-            )
+            for i in range(GROUP):
+                place = rows_of(index * GROUP + i, BACK, 0, SPAN)
+                outs[0][place, :] = result[i * SPAN : (i + 1) * SPAN]
             for i in range(tiles):
                 tile = slice(i * HEAD_DIM, (i + 1) * HEAD_DIM)
                 all_top = jnp.where(lane == index * tiles + i, top[tile], all_top)
@@ -150,23 +162,26 @@
             extra = jnp.where(row == 0, high[i : i + 1, :], low[i : i + 1, :])
             extra = extra.astype(jnp.bfloat16)
             for j in range(QUARTERS):
-                flat(outs[0])[QUARTERS * i + j, SPAN : SPAN + EXTRA, :] = extra
+                outs[0][rows_of(QUARTERS * i + j, BACK, SPAN, EXTRA), :] = extra
 
 
 def unpack_kernel(exchange, in_ref, out_ref, log_ref):
-    back = flat(in_ref)
-    for head in range(HEADS):
-        for span in range(SPANS):
+    mine = []
+    for span in range(SPANS):
+        extras = []
+        for head in range(HEADS):
+            source = SPANS * head + span
             out_ref[
                 span * SPAN : (span + 1) * SPAN, head * HEAD_DIM : (head + 1) * HEAD_DIM
-            ] = back[SPANS * head + span, 0:SPAN, :]
-    extra = back[:, SPAN : SPAN + EXTRA, :].astype(jnp.float32)
-    log_total = (extra[:, 0, :] + extra[:, 1, :]).reshape(HEADS, SPANS, HEAD_DIM)
-    mine = log_total[:, :, 0:SPAN]
-    for i in range(1, QUARTERS):
-        mine = jnp.where(quarter(exchange) == i, log_total[:, :, i * SPAN : (i + 1) * SPAN], mine)
-    for span in range(SPANS):
-        log_ref[:, span * SPAN : (span + 1) * SPAN] = mine[:, span, :]
+            ] = in_ref[rows_of(source, BACK, 0, SPAN), :]
+            terms = in_ref[rows_of(source, BACK, SPAN, EXTRA), :].astype(jnp.float32)
+            extras.append(jnp.sum(terms, axis=0, keepdims=True))
+        log_total = jnp.concatenate(extras, axis=0)
+        here = log_total[:, 0:SPAN]
+        for i in range(1, QUARTERS):
+            here = jnp.where(quarter(exchange) == i, log_total[:, i * SPAN : (i + 1) * SPAN], here)
+        mine.append(here)
+    log_ref[...] = jnp.concatenate(mine, axis=1)
 
 
 def params():
@@ -183,7 +198,7 @@
     ]
     packed = pl.pallas_call(
         functools.partial(pack_kernel, exchange),
-        out_shape=messages(3 * SPAN),
+        out_shape=messages(THERE),
         in_specs=[HBM] * 4,
         out_specs=VMEM,
         scratch_shapes=[
@@ -193,7 +208,7 @@
         ],
         compiler_params=params(),
     )(*in_hbm)
-    mine = lax.all_to_all(packed, exchange, 0, 0, tiled=True)
+    mine = exchanged(packed, exchange)
     total_rows = SOURCES * SPAN
     ring = [(i, i // parts * parts + (i + 1) % parts) for i in range(devices)]
     state = ()
@@ -201,7 +216,7 @@
     for part in range(parts):
         first, last = part == 0, part == parts - 1
         if last:
-            shapes = (messages(SPAN),)
+            shapes = (messages(BACK),)
             following = None
         else:
             shapes = (jax.ShapeDtypeStruct((total_rows, HEAD_DIM), jnp.float32),) * 3
@@ -219,7 +234,7 @@
             ),
         )(mine, other, *state)
         other = following
-    back = lax.all_to_all(state[0], exchange, 0, 0, tiled=True)
+    back = exchanged(state[0], exchange)
     return pl.pallas_call(
         functools.partial(unpack_kernel, exchange),
         out_shape=(

time: 50.7 us -> 50 us (0.986)
  Pallas kernels: 6.87 us -> 5.9 us
  transfers between devices with their start and end apart: 1 -> 1, of which waited for: 1 -> 1; matrix products, arithmetic and copies ran while one was open for 0% -> 0% of each run, Pallas kernels for 4% -> 3%
where the time goes in v4:
time: 50 us; the launch traced here: 49.8 us
  blocking collectives  42.6 us (85%)
  Pallas kernels  5.9 us (12%)
  waiting for transfers between devices  0.68 us (1%)
  between operations  0.66 us (1%)
    all_to_all x2, blocking collectives, exchanged(): lax.all_to_all(paired, exchange, 0, 0, tiled=True).reshape(array.shape)  42.6 us
    pallas_call x2, Pallas kernels, local(): pl.pallas_call(functools.partial(attend_kernel, first, last), out_shape=s...  3.69 us
    pallas_call x1, Pallas kernels, local(): pl.pallas_call(functools.partial(pack_kernel, exchange), out_shape=messag...  1.21 us
    pallas_call x1, Pallas kernels, local(): pl.pallas_call(functools.partial(unpack_kernel, exchange), out_shape=(jax...  1 us
  transfers between devices with their start and end apart: 1, of which 1 were waited for; matrix products, arithmetic and copies ran while one was open for 0% of the time, Pallas kernels for 3%

profile of v4, /device:TPU:0, one launch (start us, length us, event | category | flops | bytes accessed | tf_op | source)
XLA Modules:
  0.0 49.8 jit_solution(4246925757970541302)
XLA Ops:
  0.6 1.2 %shard_map.59 = bf16[3136,128]{1,0:T(8,128)(2,1)S(1)} custom-call(s32[2]{0:T(128)} %span_hbm.1, bf16[64,2048]{1,0:T(8,128)(2,1)} %q_hbm.1, bf16[64,2048]{1,0:T(8,128)(2,1)} %k_hbm.1, bf16[64,2048]{1,0:T(8,128)(2,1)} %v_hbm.1), custom_call_target="tpu_custom_call" | custom-call | tf_op jit(solution)/shard_map/pallas_call | solution.py:199
  1.9 28.1 %all_to_all.10 = bf16[32,49,2,128]{3,2,1,0:T(2,128)(2,1)S(1)} all-to-all(bf16[32,49,2,128]{3,2,1,0:T(2,128)(2,1)S(1)} %bitcast.8), channel_id=1, replica_groups=mesh['outer'=8,'inner'=4] {'outer','inner'}, dimensions={0} | all-to-all | bytes 1605632 | tf_op jit(solution)/shard_map/all_to_all | solution.py:42
  29.9 0.0 collective-permute-start
  29.9 1.6 %shard_map.60 = (f32[1024,128]{1,0:T(8,128)S(1)}, f32[1024,128]{1,0:T(8,128)S(1)}, f32[1024,128]{1,0:T(8,128)S(1)}) custom-call(bf16[3136,128]{1,0:T(8,128)(2,1)S(1)} %bitcast.5, bf16[3136,128]{1,0:T(8,128)(2,1)S(1)} %bitcast.6), custom_call_target="tpu_custom_call" | custom-call | flops 536870912 | bytes 1048576 | tf_op jit(solution)/shard_map/pallas_call | solution.py:224
  31.6 0.7 %collective-permute-done.other_ref = bf16[3136,128]{1,0:T(8,128)(2,1)S(1)} collective-permute-done((bf16[3136,128]{1,0:T(8,128)(2,1)S(1)}, bf16[3136,128]{1,0:T(8,128)(2,1)S(1)}, u32[]{:S(2)}, u32[]{:S(2)}) %collective-permute-start) | collective-permute-done | bytes 802848 | tf_op jit(solution)/shard_map/ppermute | solution.py:223
  32.2 2.1 %shard_map.61 = bf16[1088,128]{1,0:T(8,128)(2,1)S(1)} custom-call(bf16[3136,128]{1,0:T(8,128)(2,1)S(1)} %bitcast.7, bf16[3136,128]{1,0:T(8,128)(2,1)S(1)} %collective-permute-done.other_ref, f32[1024,128]{1,0:T(8,128)S(1)} %get-tuple-element.5.refs_0_, f32[1024,128]{1,0:T(8,128)S(1)} %get-tuple-element.6.refs_1_, f32[1024,128]{1,0:T(8,128)S(1)} %get-tuple-element.7.refs_2_), custom_call_target="tpu_custom_call" | custom-call | flops 536870912 | bytes 1048576 | tf_op jit(solution)/shard_map/pallas_call | solution.py:224
  34.3 14.5 %all_to_all.11 = bf16[32,17,2,128]{3,2,1,0:T(2,128)(2,1)S(1)} all-to-all(bf16[32,17,2,128]{3,2,1,0:T(2,128)(2,1)S(1)} %bitcast.10), channel_id=1, replica_groups=mesh['outer'=8,'inner'=4] {'outer','inner'}, dimensions={0} | all-to-all | bytes 557056 | tf_op jit(solution)/shard_map/all_to_all | solution.py:42
  48.8 1.0 %shard_map.62 = (bf16[64,2048]{1,0:T(8,128)(2,1)}, f32[16,64]{1,0:T(8,128)}) custom-call(bf16[1088,128]{1,0:T(8,128)(2,1)S(1)} %bitcast.9), custom_call_target="tpu_custom_call" | custom-call | tf_op jit(solution)/shard_map/pallas_call | solution.py:238
Async XLA Ops:
  29.9 2.3 %collective-permute-start = (bf16[3136,128]{1,0:T(8,128)(2,1)S(1)}, bf16[3136,128]{1,0:T(8,128)(2,1)S(1)}, u32[]{:S(2)}, u32[]{:S(2)}) collective-permute-start(bf16[3136,128]{1,0:T(8,128)(2,1)S(1)} %bitcast.4), channel_id=1, source_target_pairs={{0,1},{1,0},{2,3},{3,2},{4,5},{5,4},{6,7},{7,6},{8,9},{9,8},{10,11... | collective-permute-start | bytes 2408456 | tf_op jit(solution)/shard_map/ppermute | solution.py:223

commit v5 on v4

--- a/solution.py
+++ b/solution.py
@@ -20,6 +20,7 @@
 THERE = 3 * SPAN + EXTRA
 BACK = SPAN + EXTRA
 GROUP = 8
+STEP = 8
 MASKED = -1e30
 SCALE = 1.0 / math.sqrt(HEAD_DIM)
 SCALE2 = SCALE * math.log2(math.e)
@@ -90,51 +91,65 @@
     )
 
 
-def attend_kernel(first, last, mine_ref, other_ref, *refs):
+def attend_kernel(exchange, first, last, mine_ref, other_ref, *refs):
     if first:
         outs = refs
     else:
         acc_in, total_in, top_in, *outs = refs
     block = GROUP * SPAN
     blocks = SOURCES // GROUP
-    tiles = block // HEAD_DIM
-    groups = SOURCES // QUARTERS
+    tiles = SOURCES // QUARTERS
     keys = spans(other_ref, range(SOURCES), 1)
+    key_pos = positions(other_ref)
+    query_pos = key_pos if first else positions(mine_ref)
+    key_tiles = [jnp.broadcast_to(key_pos[t : t + 1, :], (STEP, HEAD_DIM)) for t in range(tiles)]
+    lane = lax.broadcasted_iota(jnp.int32, (STEP, HEAD_DIM), 1)
+    row = lax.broadcasted_iota(jnp.int32, (STEP, HEAD_DIM), 0)
 
     def score(index):
-        return lax.dot_general(
-            spans(mine_ref, range(index * GROUP, (index + 1) * GROUP), 0),
+        sources = range(index * GROUP, (index + 1) * GROUP)
+        scores = lax.dot_general(
+            spans(mine_ref, sources, 0),
             keys,
             (((1,), (1,)), ((), ())),
             preferred_element_type=jnp.float32,
         )
-
-    next_scores = score(0)
-    query_pos = jnp.concatenate([positions(mine_ref)] * (HEAD_DIM // groups), axis=0)
-    query_pos = jnp.transpose(query_pos)
-    key_pos = positions(other_ref)
-    key_row = jnp.concatenate([key_pos[i : i + 1, :] for i in range(groups)], axis=1)
+        masked = [[] for _ in range(tiles)]
+        for i, source in enumerate(sources):
+            tile, lead = source // QUARTERS, source % QUARTERS * SPAN
+            start = query_pos[tile : tile + 1, lead : lead + 1]
+            before = [key_tiles[t] < start for t in range(tiles)]
+            for j in range(0, SPAN, STEP):
+                here = i * SPAN + j
+                for t in range(tiles):
+                    visible = before[t]
+                    if first and t == tile:
+                        visible = visible | ((lane >= lead) & (lane - lead <= row + j))
+                    piece = scores[here : here + STEP, t * HEAD_DIM : (t + 1) * HEAD_DIM]
+                    masked[t].append(jnp.where(visible, piece, MASKED))
+        masked = [jnp.concatenate(pieces, axis=0) for pieces in masked]
+        return masked, jnp.max(functools.reduce(jnp.maximum, masked), axis=1, keepdims=True)
+
+    following = score(0)
     values = spans(other_ref, range(SOURCES), 2)
     values = jnp.concatenate([values, jnp.ones_like(values)], axis=1)
-    lane = lax.broadcasted_iota(jnp.int32, (HEAD_DIM, HEAD_DIM), 1)
+    square_lane = lax.broadcasted_iota(jnp.int32, (HEAD_DIM, HEAD_DIM), 1)
     all_top = jnp.zeros((HEAD_DIM, HEAD_DIM), jnp.float32)
     all_total = jnp.ones((HEAD_DIM, HEAD_DIM), jnp.float32)
     for index in range(blocks):
-        scores = next_scores
+        masked, top = following
         if index + 1 < blocks:
-            next_scores = score(index + 1)
-        query_col = jnp.concatenate(
-            [query_pos[:, index * tiles + i : index * tiles + i + 1] for i in range(tiles)], axis=0
-        )
-        scores = jnp.where(key_row <= query_col, scores, MASKED)
-        top = jnp.broadcast_to(jnp.max(scores, axis=1, keepdims=True), (block, HEAD_DIM))
+            following = score(index + 1)
         here = slice(index * block, (index + 1) * block)
+        top = jnp.broadcast_to(top, (block, HEAD_DIM))
         if not first:
             old_top = top_in[here, :]
             top = jnp.maximum(top, old_top)
             factor = jnp.exp2((old_top - top) * SCALE2)
-        weights = jnp.exp2((scores - top[:, 0:1]) * SCALE2).astype(jnp.bfloat16)
-        summed = jnp.dot(weights, values, preferred_element_type=jnp.float32)
+        weights = [jnp.exp2((piece - top) * SCALE2).astype(jnp.bfloat16) for piece in masked]
+        summed = jnp.dot(
+            jnp.concatenate(weights, axis=1), values, preferred_element_type=jnp.float32
+        )
         acc, total = summed[:, :HEAD_DIM], summed[:, HEAD_DIM:]
         if not first:
             acc = acc + acc_in[here, :] * factor
@@ -144,44 +159,44 @@
             for i in range(GROUP):
                 place = rows_of(index * GROUP + i, BACK, 0, SPAN)
                 outs[0][place, :] = result[i * SPAN : (i + 1) * SPAN]
-            for i in range(tiles):
-                tile = slice(i * HEAD_DIM, (i + 1) * HEAD_DIM)
-                all_top = jnp.where(lane == index * tiles + i, top[tile], all_top)
-                all_total = jnp.where(lane == index * tiles + i, total[tile], all_total)
+            for i in range(GROUP // QUARTERS):
+                rows = slice(i * HEAD_DIM, (i + 1) * HEAD_DIM)
+                chosen = square_lane == index * (GROUP // QUARTERS) + i
+                all_top = jnp.where(chosen, top[rows], all_top)
+                all_total = jnp.where(chosen, total[rows], all_total)
         else:
             outs[0][here, :] = acc
             outs[1][here, :] = total
             outs[2][here, :] = top
     if last:
-        log_total = jnp.transpose(all_top)[0:groups] * SCALE
-        log_total = log_total + jnp.log(jnp.transpose(all_total)[0:groups])
+        log_total = jnp.transpose(all_top)[0:tiles] * SCALE
+        log_total = log_total + jnp.log(jnp.transpose(all_total)[0:tiles])
         high = log_total.astype(jnp.bfloat16).astype(jnp.float32)
         low = log_total - high
-        row = lax.broadcasted_iota(jnp.int32, (EXTRA, HEAD_DIM), 0)
-        for i in range(groups):
-            extra = jnp.where(row == 0, high[i : i + 1, :], low[i : i + 1, :])
-            extra = extra.astype(jnp.bfloat16)
-            for j in range(QUARTERS):
-                outs[0][rows_of(QUARTERS * i + j, BACK, SPAN, EXTRA), :] = extra
-
-
-def unpack_kernel(exchange, in_ref, out_ref, log_ref):
-    mine = []
-    for span in range(SPANS):
-        extras = []
-        for head in range(HEADS):
+        span = lax.axis_index(exchange) % SPANS
+        kept = lane // SPAN == span
+        for j in range(QUARTERS):
+            shift = ((span - j) % QUARTERS) * SPAN
+            terms = [jnp.where(kept, pltpu.roll(term, shift, 1), 0.0) for term in (high, low)]
+            for i in range(tiles):
+                extra = jnp.concatenate([term[i : i + 1, :] for term in terms], axis=0)
+                outs[0][rows_of(QUARTERS * i + j, BACK, SPAN, EXTRA), :] = extra.astype(
+                    jnp.bfloat16
+                )
+
+
+def unpack_kernel(in_ref, out_ref, log_ref):
+    log_totals = []
+    for head in range(HEADS):
+        terms = 0.0
+        for span in range(SPANS):
             source = SPANS * head + span
             out_ref[
                 span * SPAN : (span + 1) * SPAN, head * HEAD_DIM : (head + 1) * HEAD_DIM
             ] = in_ref[rows_of(source, BACK, 0, SPAN), :]
-            terms = in_ref[rows_of(source, BACK, SPAN, EXTRA), :].astype(jnp.float32)
-            extras.append(jnp.sum(terms, axis=0, keepdims=True))
-        log_total = jnp.concatenate(extras, axis=0)
-        here = log_total[:, 0:SPAN]
-        for i in range(1, QUARTERS):
-            here = jnp.where(quarter(exchange) == i, log_total[:, i * SPAN : (i + 1) * SPAN], here)
-        mine.append(here)
-    log_ref[...] = jnp.concatenate(mine, axis=1)
+            terms += in_ref[rows_of(source, BACK, SPAN, EXTRA), :].astype(jnp.float32)
+        log_totals.append(terms[0:1, :] + terms[1:2, :])
+    log_ref[...] = jnp.concatenate(log_totals, axis=0)[:, 0 : SPANS * SPAN]
 
 
 def params():
@@ -222,7 +237,7 @@
             shapes = (jax.ShapeDtypeStruct((total_rows, HEAD_DIM), jnp.float32),) * 3
             following = lax.ppermute(other, everywhere, ring)
         state = pl.pallas_call(
-            functools.partial(attend_kernel, first, last),
+            functools.partial(attend_kernel, exchange, first, last),
             out_shape=shapes,
             in_specs=[VMEM] * (2 + len(state)),
             out_specs=(VMEM,) * len(shapes),
@@ -236,7 +251,7 @@
         other = following
     back = exchanged(state[0], exchange)
     return pl.pallas_call(
-        functools.partial(unpack_kernel, exchange),
+        unpack_kernel,
         out_shape=(
             jax.ShapeDtypeStruct((rows, HEADS * HEAD_DIM), jnp.bfloat16),
             jax.ShapeDtypeStruct((HEADS, rows), jnp.float32),

time: 50 us -> 49.5 us (0.990)
  Pallas kernels: 5.9 us -> 5.39 us
    pallas_call x3, Pallas kernels: 4.69 us -> 4.18 us  [the longest x2 3.4 us: local(): pl.pallas_call(functools.partial(attend_kernel, exchange, first, last), o...]
where the time goes in v5:
time: 49.5 us; the launch traced here: 49.3 us
  blocking collectives  42.6 us (86%)
  Pallas kernels  5.39 us (11%)
  waiting for transfers between devices  0.68 us (1%)
  between operations  0.66 us (1%)
    all_to_all x2, blocking collectives, exchanged(): lax.all_to_all(paired, exchange, 0, 0, tiled=True).reshape(array.shape)  42.6 us
    pallas_call x2, Pallas kernels, local(): pl.pallas_call(functools.partial(attend_kernel, exchange, first, last), o...  3.4 us
    pallas_call x1, Pallas kernels, local(): pl.pallas_call(functools.partial(pack_kernel, exchange), out_shape=messag...  1.21 us
  transfers between devices with their start and end apart: 1, of which 1 were waited for; matrix products, arithmetic and copies ran while one was open for 0% of the time, Pallas kernels for 3%

profile of v5, /device:TPU:0, one launch (start us, length us, event | category | flops | bytes accessed | tf_op | source)
XLA Modules:
  0.0 49.3 jit_solution(18421049844050341101)
XLA Ops:
  0.6 1.2 %shard_map.59 = bf16[3136,128]{1,0:T(8,128)(2,1)S(1)} custom-call(s32[2]{0:T(128)} %span_hbm.1, bf16[64,2048]{1,0:T(8,128)(2,1)} %q_hbm.1, bf16[64,2048]{1,0:T(8,128)(2,1)} %k_hbm.1, bf16[64,2048]{1,0:T(8,128)(2,1)} %v_hbm.1), custom_call_target="tpu_custom_call" | custom-call | tf_op jit(solution)/shard_map/pallas_call | solution.py:214
  1.9 28.1 %all_to_all.10 = bf16[32,49,2,128]{3,2,1,0:T(2,128)(2,1)S(1)} all-to-all(bf16[32,49,2,128]{3,2,1,0:T(2,128)(2,1)S(1)} %bitcast.8), channel_id=1, replica_groups=mesh['outer'=8,'inner'=4] {'outer','inner'}, dimensions={0} | all-to-all | bytes 1605632 | tf_op jit(solution)/shard_map/all_to_all | solution.py:43
  29.9 0.0 collective-permute-start
  29.9 1.6 %shard_map.60 = (f32[1024,128]{1,0:T(8,128)S(1)}, f32[1024,128]{1,0:T(8,128)S(1)}, f32[1024,128]{1,0:T(8,128)S(1)}) custom-call(bf16[3136,128]{1,0:T(8,128)(2,1)S(1)} %bitcast.5, bf16[3136,128]{1,0:T(8,128)(2,1)S(1)} %bitcast.6), custom_call_target="tpu_custom_call" | custom-call | flops 536870912 | bytes 1048576 | tf_op jit(solution)/shard_map/pallas_call | solution.py:239
  31.6 0.7 %collective-permute-done.other_ref = bf16[3136,128]{1,0:T(8,128)(2,1)S(1)} collective-permute-done((bf16[3136,128]{1,0:T(8,128)(2,1)S(1)}, bf16[3136,128]{1,0:T(8,128)(2,1)S(1)}, u32[]{:S(2)}, u32[]{:S(2)}) %collective-permute-start) | collective-permute-done | bytes 802848 | tf_op jit(solution)/shard_map/ppermute | solution.py:238
  32.2 1.8 %shard_map.61 = bf16[1088,128]{1,0:T(8,128)(2,1)S(1)} custom-call(bf16[3136,128]{1,0:T(8,128)(2,1)S(1)} %bitcast.7, bf16[3136,128]{1,0:T(8,128)(2,1)S(1)} %collective-permute-done.other_ref, f32[1024,128]{1,0:T(8,128)S(1)} %get-tuple-element.5.refs_0_, f32[1024,128]{1,0:T(8,128)S(1)} %get-tuple-element.6.refs_1_, f32[1024,128]{1,0:T(8,128)S(1)} %get-tuple-element.7.refs_2_), custom_call_target="tpu_custom_call" | custom-call | flops 536870912 | bytes 1048576 | tf_op jit(solution)/shard_map/pallas_call | solution.py:239
  34.0 14.5 %all_to_all.11 = bf16[32,17,2,128]{3,2,1,0:T(2,128)(2,1)S(1)} all-to-all(bf16[32,17,2,128]{3,2,1,0:T(2,128)(2,1)S(1)} %bitcast.10), channel_id=1, replica_groups=mesh['outer'=8,'inner'=4] {'outer','inner'}, dimensions={0} | all-to-all | bytes 557056 | tf_op jit(solution)/shard_map/all_to_all | solution.py:43
  48.6 0.8 %shard_map.62 = (bf16[64,2048]{1,0:T(8,128)(2,1)}, f32[16,64]{1,0:T(8,128)}) custom-call(bf16[1088,128]{1,0:T(8,128)(2,1)S(1)} %bitcast.9), custom_call_target="tpu_custom_call" | custom-call | tf_op jit(solution)/shard_map/pallas_call | solution.py:253
Async XLA Ops:
  29.9 2.3 %collective-permute-start = (bf16[3136,128]{1,0:T(8,128)(2,1)S(1)}, bf16[3136,128]{1,0:T(8,128)(2,1)S(1)}, u32[]{:S(2)}, u32[]{:S(2)}) collective-permute-start(bf16[3136,128]{1,0:T(8,128)(2,1)S(1)} %bitcast.4), channel_id=1, source_target_pairs={{0,1},{1,0},{2,3},{3,2},{4,5},{5,4},{6,7},{7,6},{8,9},{9,8},{10,11... | collective-permute-start | bytes 2408456 | tf_op jit(solution)/shard_map/ppermute | solution.py:238

commit v6 on v5

--- a/solution.py
+++ b/solution.py
@@ -21,6 +21,11 @@
 BACK = SPAN + EXTRA
 GROUP = 8
 STEP = 8
+THERE_ORDER = (
+    0, 8, 16, 24, 2, 10, 18, 26, 1, 9, 17, 25, 3, 11, 19, 27, 4, 12, 20, 28, 6, 14, 22, 30, 5,
+    13, 21, 29, 7, 15, 23, 31,
+)
+BACK_ORDER = THERE_ORDER
 MASKED = -1e30
 SCALE = 1.0 / math.sqrt(HEAD_DIM)
 SCALE2 = SCALE * math.log2(math.e)
@@ -38,16 +43,18 @@
     return jax.ShapeDtypeStruct((SOURCES * size, HEAD_DIM), jnp.bfloat16)
 
 
-def exchanged(array, exchange):
+def exchanged(array, order):
+    parts = lax.axis_size("source") // HEADS
+    groups = [
+        [member // SPANS * parts + first + member % SPANS for member in order]
+        for first in range(0, parts, SPANS)
+    ]
     paired = array.reshape(SOURCES, -1, 2, HEAD_DIM)
-    return lax.all_to_all(paired, exchange, 0, 0, tiled=True).reshape(array.shape)
-
-
-def quarter(exchange):
-    return lax.axis_index(exchange) % QUARTERS
-
-
-def pack_kernel(exchange, span_hbm, q_hbm, k_hbm, v_hbm, out_ref, ranks, buffers, sems):
+    paired = lax.all_to_all(paired, "source", 0, 0, axis_index_groups=groups, tiled=True)
+    return paired.reshape(array.shape)
+
+
+def pack_kernel(span_hbm, q_hbm, k_hbm, v_hbm, out_ref, ranks, buffers, sems):
     span_copy = pltpu.make_async_copy(span_hbm, ranks, sems.at[3])
     span_copy.start()
     copies = [
@@ -57,28 +64,30 @@
     for copy in copies:
         copy.start()
     span_copy.wait()
-    lane = lax.broadcasted_iota(jnp.int32, (EXTRA, HEAD_DIM), 1)
     row = lax.broadcasted_iota(jnp.int32, (EXTRA, HEAD_DIM), 0)
+    digits = []
     for span in range(SPANS):
         digit = jnp.where(row == 0, ranks[span] // DIGIT, ranks[span] % DIGIT)
-        extra = jnp.where(lane // SPAN == quarter(exchange), digit, 0)
-        extra = extra.astype(jnp.float32).astype(jnp.bfloat16)
-        for head in range(HEADS):
-            out_ref[rows_of(SPANS * head + span, THERE, 3 * SPAN, EXTRA), :] = extra
+        digits.append(digit.astype(jnp.float32).astype(jnp.bfloat16))
+    for place, member in enumerate(THERE_ORDER):
+        out_ref[rows_of(place, THERE, 3 * SPAN, EXTRA), :] = digits[member % SPANS]
     for i, copy in enumerate(copies):
         copy.wait()
-        for head in range(HEADS):
-            for span in range(SPANS):
-                out_ref[rows_of(SPANS * head + span, THERE, i * SPAN, SPAN), :] = buffers[
-                    i, span * SPAN : (span + 1) * SPAN, head * HEAD_DIM : (head + 1) * HEAD_DIM
-                ]
+        for place, member in enumerate(THERE_ORDER):
+            head, span = member // SPANS, member % SPANS
+            out_ref[rows_of(place, THERE, i * SPAN, SPAN), :] = buffers[
+                i, span * SPAN : (span + 1) * SPAN, head * HEAD_DIM : (head + 1) * HEAD_DIM
+            ]
 
 
 def positions(ref):
+    lane = lax.broadcasted_iota(jnp.int32, (EXTRA, HEAD_DIM), 1)
     ranks = []
     for i in range(0, SOURCES, QUARTERS):
-        extras = [ref[rows_of(i + j, THERE, 3 * SPAN, EXTRA), :] for j in range(QUARTERS)]
-        digits = sum(extra.astype(jnp.float32) for extra in extras)
+        digits = 0.0
+        for j in range(QUARTERS):
+            extra = ref[rows_of(i + j, THERE, 3 * SPAN, EXTRA), :].astype(jnp.float32)
+            digits = jnp.where(lane // SPAN == j, extra, digits)
         ranks.append(digits[0:1] * DIGIT + digits[1:2])
     rank = jnp.concatenate(ranks, axis=0)
     lane = lax.broadcasted_iota(jnp.int32, rank.shape, 1)
@@ -91,7 +100,11 @@
     )
 
 
-def attend_kernel(exchange, first, last, mine_ref, other_ref, *refs):
+def home(source):
+    return BACK_ORDER.index(THERE_ORDER[source])
+
+
+def attend_kernel(first, last, mine_ref, other_ref, *refs):
     if first:
         outs = refs
     else:
@@ -157,8 +170,7 @@
         if last:
             result = (acc * (1.0 / total)).astype(jnp.bfloat16)
             for i in range(GROUP):
-                place = rows_of(index * GROUP + i, BACK, 0, SPAN)
-                outs[0][place, :] = result[i * SPAN : (i + 1) * SPAN]
+                outs[0][rows_of(home(index * GROUP + i), BACK, 0, SPAN), :] = result[i * SPAN : (i + 1) * SPAN]
             for i in range(GROUP // QUARTERS):
                 rows = slice(i * HEAD_DIM, (i + 1) * HEAD_DIM)
                 chosen = square_lane == index * (GROUP // QUARTERS) + i
@@ -173,16 +185,15 @@
         log_total = log_total + jnp.log(jnp.transpose(all_total)[0:tiles])
         high = log_total.astype(jnp.bfloat16).astype(jnp.float32)
         low = log_total - high
-        span = lax.axis_index(exchange) % SPANS
+        span = lax.axis_index("source") % SPANS
         kept = lane // SPAN == span
         for j in range(QUARTERS):
             shift = ((span - j) % QUARTERS) * SPAN
             terms = [jnp.where(kept, pltpu.roll(term, shift, 1), 0.0) for term in (high, low)]
             for i in range(tiles):
                 extra = jnp.concatenate([term[i : i + 1, :] for term in terms], axis=0)
-                outs[0][rows_of(QUARTERS * i + j, BACK, SPAN, EXTRA), :] = extra.astype(
-                    jnp.bfloat16
-                )
+                place = rows_of(home(QUARTERS * i + j), BACK, SPAN, EXTRA)
+                outs[0][place, :] = extra.astype(jnp.bfloat16)
 
 
 def unpack_kernel(in_ref, out_ref, log_ref):
@@ -190,7 +201,7 @@
     for head in range(HEADS):
         terms = 0.0
         for span in range(SPANS):
-            source = SPANS * head + span
+            source = BACK_ORDER.index(SPANS * head + span)
             out_ref[
                 span * SPAN : (span + 1) * SPAN, head * HEAD_DIM : (head + 1) * HEAD_DIM
             ] = in_ref[rows_of(source, BACK, 0, SPAN), :]
@@ -203,16 +214,16 @@
     return pltpu.CompilerParams(vmem_limit_bytes=VMEM_LIMIT)
 
 
-def local(everywhere, exchange, queries, keys, values, span_order):
+def local(queries, keys, values, span_order):
     rows = queries.shape[0]
-    devices = lax.axis_size(everywhere)
+    devices = lax.axis_size("source")
     parts = devices // HEADS
     in_hbm = [
         pltpu.with_memory_space_constraint(array, pltpu.HBM)
         for array in (span_order, queries, keys, values)
     ]
     packed = pl.pallas_call(
-        functools.partial(pack_kernel, exchange),
+        pack_kernel,
         out_shape=messages(THERE),
         in_specs=[HBM] * 4,
         out_specs=VMEM,
@@ -223,7 +234,7 @@
         ],
         compiler_params=params(),
     )(*in_hbm)
-    mine = exchanged(packed, exchange)
+    mine = exchanged(packed, THERE_ORDER)
     total_rows = SOURCES * SPAN
     ring = [(i, i // parts * parts + (i + 1) % parts) for i in range(devices)]
     state = ()
@@ -235,9 +246,9 @@
             following = None
         else:
             shapes = (jax.ShapeDtypeStruct((total_rows, HEAD_DIM), jnp.float32),) * 3
-            following = lax.ppermute(other, everywhere, ring)
+            following = lax.ppermute(other, "source", ring)
         state = pl.pallas_call(
-            functools.partial(attend_kernel, exchange, first, last),
+            functools.partial(attend_kernel, first, last),
             out_shape=shapes,
             in_specs=[VMEM] * (2 + len(state)),
             out_specs=(VMEM,) * len(shapes),
@@ -249,7 +260,7 @@
             ),
         )(mine, other, *state)
         other = following
-    back = exchanged(state[0], exchange)
+    back = exchanged(state[0], BACK_ORDER)
     return pl.pallas_call(
         unpack_kernel,
         out_shape=(
@@ -263,16 +274,11 @@
 
 
 def solution(mesh):
-    devices = mesh.devices.reshape(HEADS, -1, SPANS)
-    if devices.shape[1] == 1:
-        devices, everywhere, exchange = devices.reshape(-1), ("source",), ("source",)
-    else:
-        everywhere, exchange = ("head", "ring", "core"), ("head", "core")
-    rows = P(everywhere, None)
+    rows = P("source", None)
     return jax.shard_map(
-        functools.partial(local, everywhere, exchange),
-        mesh=Mesh(devices, everywhere),
-        in_specs=(rows, rows, rows, P(everywhere)),
-        out_specs=(rows, P(None, everywhere)),
+        local,
+        mesh=Mesh(mesh.devices.reshape(-1), ("source",)),
+        in_specs=(rows, rows, rows, P("source")),
+        out_specs=(rows, P(None, "source")),
         check_vma=False,
     )

time: 49.5 us -> 48.7 us (0.984)
  blocking collectives: 42.6 us -> 41.8 us
    all_to_all x2, blocking collectives: 42.6 us -> 41.8 us  [exchanged(): lax.all_to_all(paired, 'source', 0, 0, axis_index_groups=groups, tiled=True)]
where the time goes in v6:
time: 48.7 us; the launch traced here: 48.5 us
  blocking collectives  41.8 us (86%)
  Pallas kernels  5.39 us (11%)
  waiting for transfers between devices  0.68 us (1%)
  between operations  0.66 us (1%)
    all_to_all x2, blocking collectives, exchanged(): lax.all_to_all(paired, 'source', 0, 0, axis_index_groups=groups, tiled=True)  41.8 us
    pallas_call x2, Pallas kernels, local(): pl.pallas_call(functools.partial(attend_kernel, first, last), out_shape=s...  3.4 us
    pallas_call x1, Pallas kernels, local(): pl.pallas_call(pack_kernel, out_shape=messages(THERE), in_specs=[HBM] * 4...  1.21 us
  transfers between devices with their start and end apart: 1, of which 1 were waited for; matrix products, arithmetic and copies ran while one was open for 0% of the time, Pallas kernels for 3%

profile of v6, /device:TPU:0, one launch (start us, length us, event | category | flops | bytes accessed | tf_op | source)
XLA Modules:
  0.0 48.5 jit_solution(11215312832556352233)
XLA Ops:
  0.6 1.2 %shard_map.59 = bf16[3136,128]{1,0:T(8,128)(2,1)S(1)} custom-call(s32[2]{0:T(128)} %span_hbm.1, bf16[64,2048]{1,0:T(8,128)(2,1)} %q_hbm.1, bf16[64,2048]{1,0:T(8,128)(2,1)} %k_hbm.1, bf16[64,2048]{1,0:T(8,128)(2,1)} %v_hbm.1), custom_call_target="tpu_custom_call" | custom-call | tf_op jit(solution)/shard_map/pallas_call | solution.py:225
  1.9 28.8 %all_to_all.10 = bf16[32,49,2,128]{3,2,1,0:T(2,128)(2,1)S(1)} all-to-all(bf16[32,49,2,128]{3,2,1,0:T(2,128)(2,1)S(1)} %bitcast.8), channel_id=1, replica_groups={{0,8,16,24,2,10,18,26,1,9,17,25,3,11,19,27,4,12,20,28,6,14,22,30,5,13,2..., dimensions={0} | all-to-all | bytes 1605632 | tf_op jit(solution)/shard_map/all_to_all | solution.py:53
  30.7 0.0 collective-permute-start
  30.7 1.6 %shard_map.60 = (f32[1024,128]{1,0:T(8,128)S(1)}, f32[1024,128]{1,0:T(8,128)S(1)}, f32[1024,128]{1,0:T(8,128)S(1)}) custom-call(bf16[3136,128]{1,0:T(8,128)(2,1)S(1)} %bitcast.5, bf16[3136,128]{1,0:T(8,128)(2,1)S(1)} %bitcast.6), custom_call_target="tpu_custom_call" | custom-call | flops 536870912 | bytes 1048576 | tf_op jit(solution)/shard_map/pallas_call | solution.py:250
  32.3 0.7 %collective-permute-done.other_ref = bf16[3136,128]{1,0:T(8,128)(2,1)S(1)} collective-permute-done((bf16[3136,128]{1,0:T(8,128)(2,1)S(1)}, bf16[3136,128]{1,0:T(8,128)(2,1)S(1)}, u32[]{:S(2)}, u32[]{:S(2)}) %collective-permute-start) | collective-permute-done | bytes 802848 | tf_op jit(solution)/shard_map/ppermute | solution.py:249
  33.0 1.8 %shard_map.61 = bf16[1088,128]{1,0:T(8,128)(2,1)S(1)} custom-call(bf16[3136,128]{1,0:T(8,128)(2,1)S(1)} %bitcast.7, bf16[3136,128]{1,0:T(8,128)(2,1)S(1)} %collective-permute-done.other_ref, f32[1024,128]{1,0:T(8,128)S(1)} %get-tuple-element.5.refs_0_, f32[1024,128]{1,0:T(8,128)S(1)} %get-tuple-element.6.refs_1_, f32[1024,128]{1,0:T(8,128)S(1)} %get-tuple-element.7.refs_2_), custom_call_target="tpu_custom_call" | custom-call | flops 536870912 | bytes 1048576 | tf_op jit(solution)/shard_map/pallas_call | solution.py:250
  34.8 13.0 %all_to_all.11 = bf16[32,17,2,128]{3,2,1,0:T(2,128)(2,1)S(1)} all-to-all(bf16[32,17,2,128]{3,2,1,0:T(2,128)(2,1)S(1)} %bitcast.10), channel_id=1, replica_groups={{0,8,16,24,2,10,18,26,1,9,17,25,3,11,19,27,4,12,20,28,6,14,22,30,5,13,2..., dimensions={0} | all-to-all | bytes 557056 | tf_op jit(solution)/shard_map/all_to_all | solution.py:53
  47.7 0.8 %shard_map.62 = (bf16[64,2048]{1,0:T(8,128)(2,1)}, f32[16,64]{1,0:T(8,128)}) custom-call(bf16[1088,128]{1,0:T(8,128)(2,1)S(1)} %bitcast.9), custom_call_target="tpu_custom_call" | custom-call | tf_op jit(solution)/shard_map/pallas_call | solution.py:264
Async XLA Ops:
  30.7 2.3 %collective-permute-start = (bf16[3136,128]{1,0:T(8,128)(2,1)S(1)}, bf16[3136,128]{1,0:T(8,128)(2,1)S(1)}, u32[]{:S(2)}, u32[]{:S(2)}) collective-permute-start(bf16[3136,128]{1,0:T(8,128)(2,1)S(1)} %bitcast.4), channel_id=1, source_target_pairs={{0,1},{1,0},{2,3},{3,2},{4,5},{5,4},{6,7},{7,6},{8,9},{9,8},{10,11... | collective-permute-start | bytes 2408456 | tf_op jit(solution)/shard_map/ppermute | solution.py:249

commit v7 on v6

--- a/solution.py
+++ b/solution.py
@@ -25,7 +25,10 @@
     0, 8, 16, 24, 2, 10, 18, 26, 1, 9, 17, 25, 3, 11, 19, 27, 4, 12, 20, 28, 6, 14, 22, 30, 5,
     13, 21, 29, 7, 15, 23, 31,
 )
-BACK_ORDER = THERE_ORDER
+BACK_ORDER = (
+    1, 31, 23, 15, 7, 29, 21, 13, 5, 30, 22, 0, 6, 28, 20, 12, 4, 27, 19, 11, 24, 26, 25, 14,
+    9, 3, 18, 10, 17, 16, 8, 2,
+)
 MASKED = -1e30
 SCALE = 1.0 / math.sqrt(HEAD_DIM)
 SCALE2 = SCALE * math.log2(math.e)

time: 48.7 us -> 47.2 us (0.969)
  blocking collectives: 41.8 us -> 40.3 us
    all_to_all x2, blocking collectives: 41.8 us -> 40.3 us  [exchanged(): lax.all_to_all(paired, 'source', 0, 0, axis_index_groups=groups, tiled=True)]
where the time goes in v7:
time: 47.2 us; the launch traced here: 47.1 us
  blocking collectives  40.3 us (85%)
  Pallas kernels  5.39 us (11%)
  waiting for transfers between devices  0.68 us (1%)
  between operations  0.66 us (1%)
    all_to_all x2, blocking collectives, exchanged(): lax.all_to_all(paired, 'source', 0, 0, axis_index_groups=groups, tiled=True)  40.3 us
    pallas_call x2, Pallas kernels, local(): pl.pallas_call(functools.partial(attend_kernel, first, last), out_shape=s...  3.39 us
    pallas_call x1, Pallas kernels, local(): pl.pallas_call(pack_kernel, out_shape=messages(THERE), in_specs=[HBM] * 4...  1.21 us
  transfers between devices with their start and end apart: 1, of which 1 were waited for; matrix products, arithmetic and copies ran while one was open for 0% of the time, Pallas kernels for 3%

profile of v7, /device:TPU:0, one launch (start us, length us, event | category | flops | bytes accessed | tf_op | source)
XLA Modules:
  0.0 47.1 jit_solution(14258991686872815238)
XLA Ops:
  0.6 1.2 %shard_map.59 = bf16[3136,128]{1,0:T(8,128)(2,1)S(1)} custom-call(s32[2]{0:T(128)} %span_hbm.1, bf16[64,2048]{1,0:T(8,128)(2,1)} %q_hbm.1, bf16[64,2048]{1,0:T(8,128)(2,1)} %k_hbm.1, bf16[64,2048]{1,0:T(8,128)(2,1)} %v_hbm.1), custom_call_target="tpu_custom_call" | custom-call | tf_op jit(solution)/shard_map/pallas_call | solution.py:228
  1.9 28.8 %all_to_all.10 = bf16[32,49,2,128]{3,2,1,0:T(2,128)(2,1)S(1)} all-to-all(bf16[32,49,2,128]{3,2,1,0:T(2,128)(2,1)S(1)} %bitcast.8), channel_id=1, replica_groups={{0,8,16,24,2,10,18,26,1,9,17,25,3,11,19,27,4,12,20,28,6,14,22,30,5,13,2..., dimensions={0} | all-to-all | bytes 1605632 | tf_op jit(solution)/shard_map/all_to_all | solution.py:56
  30.7 0.0 collective-permute-start
  30.7 1.6 %shard_map.60 = (f32[1024,128]{1,0:T(8,128)S(1)}, f32[1024,128]{1,0:T(8,128)S(1)}, f32[1024,128]{1,0:T(8,128)S(1)}) custom-call(bf16[3136,128]{1,0:T(8,128)(2,1)S(1)} %bitcast.5, bf16[3136,128]{1,0:T(8,128)(2,1)S(1)} %bitcast.6), custom_call_target="tpu_custom_call" | custom-call | flops 536870912 | bytes 1048576 | tf_op jit(solution)/shard_map/pallas_call | solution.py:253
  32.3 0.7 %collective-permute-done.other_ref = bf16[3136,128]{1,0:T(8,128)(2,1)S(1)} collective-permute-done((bf16[3136,128]{1,0:T(8,128)(2,1)S(1)}, bf16[3136,128]{1,0:T(8,128)(2,1)S(1)}, u32[]{:S(2)}, u32[]{:S(2)}) %collective-permute-start) | collective-permute-done | bytes 802848 | tf_op jit(solution)/shard_map/ppermute | solution.py:252
  33.0 1.8 %shard_map.61 = bf16[1088,128]{1,0:T(8,128)(2,1)S(1)} custom-call(bf16[3136,128]{1,0:T(8,128)(2,1)S(1)} %bitcast.7, bf16[3136,128]{1,0:T(8,128)(2,1)S(1)} %collective-permute-done.other_ref, f32[1024,128]{1,0:T(8,128)S(1)} %get-tuple-element.5.refs_0_, f32[1024,128]{1,0:T(8,128)S(1)} %get-tuple-element.6.refs_1_, f32[1024,128]{1,0:T(8,128)S(1)} %get-tuple-element.7.refs_2_), custom_call_target="tpu_custom_call" | custom-call | flops 536870912 | bytes 1048576 | tf_op jit(solution)/shard_map/pallas_call | solution.py:253
  34.8 11.5 %all_to_all.11 = bf16[32,17,2,128]{3,2,1,0:T(2,128)(2,1)S(1)} all-to-all(bf16[32,17,2,128]{3,2,1,0:T(2,128)(2,1)S(1)} %bitcast.10), channel_id=1, replica_groups={{1,31,23,15,7,29,21,13,5,30,22,0,6,28,20,12,4,27,19,11,24,26,25,14,9,3,..., dimensions={0} | all-to-all | bytes 557056 | tf_op jit(solution)/shard_map/all_to_all | solution.py:56
  46.3 0.8 %shard_map.62 = (bf16[64,2048]{1,0:T(8,128)(2,1)}, f32[16,64]{1,0:T(8,128)}) custom-call(bf16[1088,128]{1,0:T(8,128)(2,1)S(1)} %bitcast.9), custom_call_target="tpu_custom_call" | custom-call | tf_op jit(solution)/shard_map/pallas_call | solution.py:267
Async XLA Ops:
  30.7 2.3 %collective-permute-start = (bf16[3136,128]{1,0:T(8,128)(2,1)S(1)}, bf16[3136,128]{1,0:T(8,128)(2,1)S(1)}, u32[]{:S(2)}, u32[]{:S(2)}) collective-permute-start(bf16[3136,128]{1,0:T(8,128)(2,1)S(1)} %bitcast.4), channel_id=1, source_target_pairs={{0,1},{1,0},{2,3},{3,2},{4,5},{5,4},{6,7},{7,6},{8,9},{9,8},{10,11... | collective-permute-start | bytes 2408456 | tf_op jit(solution)/shard_map/ppermute | solution.py:252

commit v8 on v7

--- a/solution.py
+++ b/solution.py
@@ -19,7 +19,8 @@
 EXTRA = 2
 THERE = 3 * SPAN + EXTRA
 BACK = SPAN + EXTRA
-GROUP = 8
+KEYS = SOURCES * SPAN
+GROUP = 16
 STEP = 8
 THERE_ORDER = (
     0, 8, 16, 24, 2, 10, 18, 26, 1, 9, 17, 25, 3, 11, 19, 27, 4, 12, 20, 28, 6, 14, 22, 30, 5,
@@ -83,13 +84,22 @@
             ]
 
 
+def sort_kernel(in_ref, queries_ref, others_ref):
+    for source in range(SOURCES):
+        for which, ref, start in ((1, others_ref, 0), (2, others_ref, KEYS), (0, queries_ref, 0)):
+            place = rows_of(source, SPAN, start, SPAN)
+            ref[place, :] = in_ref[rows_of(source, THERE, which * SPAN, SPAN), :]
+        place = rows_of(source, EXTRA, 2 * KEYS, EXTRA)
+        others_ref[place, :] = in_ref[rows_of(source, THERE, 3 * SPAN, EXTRA), :]
+
+
 def positions(ref):
     lane = lax.broadcasted_iota(jnp.int32, (EXTRA, HEAD_DIM), 1)
     ranks = []
     for i in range(0, SOURCES, QUARTERS):
         digits = 0.0
         for j in range(QUARTERS):
-            extra = ref[rows_of(i + j, THERE, 3 * SPAN, EXTRA), :].astype(jnp.float32)
+            extra = ref[rows_of(i + j, EXTRA, 2 * KEYS, EXTRA), :].astype(jnp.float32)
             digits = jnp.where(lane // SPAN == j, extra, digits)
         ranks.append(digits[0:1] * DIGIT + digits[1:2])
     rank = jnp.concatenate(ranks, axis=0)
@@ -97,17 +107,11 @@
     return rank * SPAN + (lane % SPAN).astype(jnp.float32)
 
 
-def spans(ref, sources, which):
-    return jnp.concatenate(
-        [ref[rows_of(source, THERE, which * SPAN, SPAN), :] for source in sources], axis=0
-    )
-
-
 def home(source):
     return BACK_ORDER.index(THERE_ORDER[source])
 
 
-def attend_kernel(first, last, mine_ref, other_ref, *refs):
+def attend_kernel(first, last, query_ref, mine_ref, other_ref, *refs):
     if first:
         outs = refs
     else:
@@ -115,7 +119,7 @@
     block = GROUP * SPAN
     blocks = SOURCES // GROUP
     tiles = SOURCES // QUARTERS
-    keys = spans(other_ref, range(SOURCES), 1)
+    keys = other_ref[0:KEYS, :]
     key_pos = positions(other_ref)
     query_pos = key_pos if first else positions(mine_ref)
     key_tiles = [jnp.broadcast_to(key_pos[t : t + 1, :], (STEP, HEAD_DIM)) for t in range(tiles)]
@@ -125,7 +129,7 @@
     def score(index):
         sources = range(index * GROUP, (index + 1) * GROUP)
         scores = lax.dot_general(
-            spans(mine_ref, sources, 0),
+            query_ref[index * block : (index + 1) * block, :],
             keys,
             (((1,), (1,)), ((), ())),
             preferred_element_type=jnp.float32,
@@ -147,7 +151,7 @@
         return masked, jnp.max(functools.reduce(jnp.maximum, masked), axis=1, keepdims=True)
 
     following = score(0)
-    values = spans(other_ref, range(SOURCES), 2)
+    values = other_ref[KEYS : 2 * KEYS, :]
     values = jnp.concatenate([values, jnp.ones_like(values)], axis=1)
     square_lane = lax.broadcasted_iota(jnp.int32, (HEAD_DIM, HEAD_DIM), 1)
     all_top = jnp.zeros((HEAD_DIM, HEAD_DIM), jnp.float32)
@@ -237,8 +241,16 @@
         ],
         compiler_params=params(),
     )(*in_hbm)
-    mine = exchanged(packed, THERE_ORDER)
-    total_rows = SOURCES * SPAN
+    queries, mine = pl.pallas_call(
+        sort_kernel,
+        out_shape=(
+            jax.ShapeDtypeStruct((KEYS, HEAD_DIM), jnp.bfloat16),
+            jax.ShapeDtypeStruct((2 * KEYS + SOURCES * EXTRA, HEAD_DIM), jnp.bfloat16),
+        ),
+        in_specs=[VMEM],
+        out_specs=(VMEM, VMEM),
+        compiler_params=params(),
+    )(exchanged(packed, THERE_ORDER))
     ring = [(i, i // parts * parts + (i + 1) % parts) for i in range(devices)]
     state = ()
     other = mine
@@ -248,20 +260,20 @@
             shapes = (messages(BACK),)
             following = None
         else:
-            shapes = (jax.ShapeDtypeStruct((total_rows, HEAD_DIM), jnp.float32),) * 3
+            shapes = (jax.ShapeDtypeStruct((KEYS, HEAD_DIM), jnp.float32),) * 3
             following = lax.ppermute(other, "source", ring)
         state = pl.pallas_call(
             functools.partial(attend_kernel, first, last),
             out_shape=shapes,
-            in_specs=[VMEM] * (2 + len(state)),
+            in_specs=[VMEM] * (3 + len(state)),
             out_specs=(VMEM,) * len(shapes),
             compiler_params=params(),
             cost_estimate=pl.CostEstimate(
-                flops=4 * total_rows * total_rows * HEAD_DIM,
+                flops=4 * KEYS * KEYS * HEAD_DIM,
                 bytes_accessed=1 << 20,
-                transcendentals=total_rows * total_rows,
+                transcendentals=KEYS * KEYS,
             ),
-        )(mine, other, *state)
+        )(queries, mine, other, *state)
         other = following
     back = exchanged(state[0], BACK_ORDER)
     return pl.pallas_call(

time: 47.2 us -> 47.1 us (level)
  no operation moved by 1% of the time
where the time goes in v8:
time: 47.1 us; the launch traced here: 46.9 us
  blocking collectives  40.4 us (86%)
  Pallas kernels  5.5 us (12%)
  between operations  0.67 us (1%)
    all_to_all x2, blocking collectives, exchanged(): lax.all_to_all(paired, 'source', 0, 0, axis_index_groups=groups, tiled=True)  40.4 us
    pallas_call x2, Pallas kernels, local(): pl.pallas_call(functools.partial(attend_kernel, first, last), out_shape=s...  3.31 us
    pallas_call x1, Pallas kernels, local(): pl.pallas_call(pack_kernel, out_shape=messages(THERE), in_specs=[HBM] * 4...  1.21 us
  transfers between devices with their start and end apart: 1, of which 1 were waited for; matrix products, arithmetic and copies ran while one was open for 0% of the time, Pallas kernels for 3%

profile of v8, /device:TPU:0, one launch (start us, length us, event | category | flops | bytes accessed | tf_op | source)
XLA Modules:
  0.0 46.9 jit_solution(2232716424447973984)
XLA Ops:
  0.6 1.2 %shard_map.59 = bf16[3136,128]{1,0:T(8,128)(2,1)S(1)} custom-call(s32[2]{0:T(128)} %span_hbm.1, bf16[64,2048]{1,0:T(8,128)(2,1)} %q_hbm.1, bf16[64,2048]{1,0:T(8,128)(2,1)} %k_hbm.1, bf16[64,2048]{1,0:T(8,128)(2,1)} %v_hbm.1), custom_call_target="tpu_custom_call" | custom-call | tf_op jit(solution)/shard_map/pallas_call | solution.py:232
  1.9 28.8 %all_to_all.10 = bf16[32,49,2,128]{3,2,1,0:T(2,128)(2,1)S(1)} all-to-all(bf16[32,49,2,128]{3,2,1,0:T(2,128)(2,1)S(1)} %bitcast.5), channel_id=1, replica_groups={{0,8,16,24,2,10,18,26,1,9,17,25,3,11,19,27,4,12,20,28,6,14,22,30,5,13,2..., dimensions={0} | all-to-all | bytes 1605632 | tf_op jit(solution)/shard_map/all_to_all | solution.py:57
  30.7 0.2 shard_map.60
  30.9 0.1 collective-permute-start
  31.0 1.6 %shard_map.61 = (f32[1024,128]{1,0:T(8,128)S(1)}, f32[1024,128]{1,0:T(8,128)S(1)}, f32[1024,128]{1,0:T(8,128)S(1)}) custom-call(bf16[1024,128]{1,0:T(8,128)(2,1)S(1)} %get-tuple-element.7.query_ref, bf16[2112,128]{1,0:T(8,128)(2,1)S(1)} %get-tuple-element.8.mine_ref.other_ref, bf16[2112,128]{1,0:T(8,128)(2,1)S(1)} %get-tuple-element.8.mine_ref.other_ref), custom_call_target="tpu_custom_call" | custom-call | flops 536870912 | bytes 1048576 | tf_op jit(solution)/shard_map/pallas_call | solution.py:265
  32.5 0.3 collective-permute-done.other_ref
  32.9 1.7 %shard_map.62 = bf16[1088,128]{1,0:T(8,128)(2,1)S(1)} custom-call(bf16[1024,128]{1,0:T(8,128)(2,1)S(1)} %get-tuple-element.7.query_ref, bf16[2112,128]{1,0:T(8,128)(2,1)S(1)} %get-tuple-element.8.mine_ref.other_ref, bf16[2112,128]{1,0:T(8,128)(2,1)S(1)} %collective-permute-done.other_ref, f32[1024,128]{1,0:T(8,128)S(1)} %get-tuple-element.9.refs_0_, ...), custom_call_target="tpu_custom_call" | custom-call | flops 536870912 | bytes 1048576 | tf_op jit(solution)/shard_map/pallas_call | solution.py:265
  34.6 11.5 %all_to_all.11 = bf16[32,17,2,128]{3,2,1,0:T(2,128)(2,1)S(1)} all-to-all(bf16[32,17,2,128]{3,2,1,0:T(2,128)(2,1)S(1)} %bitcast.6), channel_id=1, replica_groups={{1,31,23,15,7,29,21,13,5,30,22,0,6,28,20,12,4,27,19,11,24,26,25,14,9,3,..., dimensions={0} | all-to-all | bytes 557056 | tf_op jit(solution)/shard_map/all_to_all | solution.py:57
  46.2 0.8 %shard_map.63 = (bf16[64,2048]{1,0:T(8,128)(2,1)}, f32[16,64]{1,0:T(8,128)}) custom-call(bf16[1088,128]{1,0:T(8,128)(2,1)S(1)} %bitcast.7), custom_call_target="tpu_custom_call" | custom-call | tf_op jit(solution)/shard_map/pallas_call | solution.py:279
Async XLA Ops:
  30.9 2.0 %collective-permute-start = (bf16[2112,128]{1,0:T(8,128)(2,1)S(1)}, bf16[2112,128]{1,0:T(8,128)(2,1)S(1)}, u32[]{:S(2)}, u32[]{:S(2)}) collective-permute-start(bf16[2112,128]{1,0:T(8,128)(2,1)S(1)} %get-tuple-element.8.mine_ref.other_ref), channel_id=1, source_target_pairs={{0,1},{1,0},{2,3},{3,2},{4,5},{5,4},{6,7},{7,6},{8,9},{9,8},{10,11... | collective-permute-start | bytes 1622024 | tf_op jit(solution)/shard_map/ppermute | solution.py:264

commit v9 on v8

--- a/solution.py
+++ b/solution.py
@@ -23,12 +23,12 @@
 GROUP = 16
 STEP = 8
 THERE_ORDER = (
-    0, 8, 16, 24, 2, 10, 18, 26, 1, 9, 17, 25, 3, 11, 19, 27, 4, 12, 20, 28, 6, 14, 22, 30, 5,
-    13, 21, 29, 7, 15, 23, 31,
+    0, 16, 24, 8, 10, 26, 18, 2, 1, 17, 25, 9, 11, 27, 19, 3, 4, 20, 28, 12, 14, 30, 22, 6, 5,
+    21, 29, 13, 15, 31, 23, 7,
 )
 BACK_ORDER = (
-    1, 31, 23, 15, 7, 29, 21, 13, 5, 30, 22, 0, 6, 28, 20, 12, 4, 27, 19, 11, 24, 26, 25, 14,
-    9, 3, 18, 10, 17, 16, 8, 2,
+    1, 31, 11, 15, 7, 29, 21, 30, 5, 13, 22, 0, 6, 28, 20, 12, 4, 27, 19, 23, 24, 26, 25, 14,
+    9, 3, 18, 10, 17, 2, 8, 16,
 )
 MASKED = -1e30
 SCALE = 1.0 / math.sqrt(HEAD_DIM)

time: 47.1 us -> 47.1 us (level)
  no operation moved by 1% of the time
where the time goes in v9:
time: 47.1 us; the launch traced here: 46.6 us
  blocking collectives  40 us (85%)
  Pallas kernels  5.5 us (12%)
  between operations  0.67 us (1%)
    all_to_all x2, blocking collectives, exchanged(): lax.all_to_all(paired, 'source', 0, 0, axis_index_groups=groups, tiled=True)  40 us
    pallas_call x2, Pallas kernels, local(): pl.pallas_call(functools.partial(attend_kernel, first, last), out_shape=s...  3.31 us
    pallas_call x1, Pallas kernels, local(): pl.pallas_call(pack_kernel, out_shape=messages(THERE), in_specs=[HBM] * 4...  1.21 us
  transfers between devices with their start and end apart: 1, of which 1 were waited for; matrix products, arithmetic and copies ran while one was open for 0% of the time, Pallas kernels for 3%

profile of v9, /device:TPU:0, one launch (start us, length us, event | category | flops | bytes accessed | tf_op | source)
XLA Modules:
  0.0 46.6 jit_solution(13565596307718882244)
XLA Ops:
  0.6 1.2 %shard_map.59 = bf16[3136,128]{1,0:T(8,128)(2,1)S(1)} custom-call(s32[2]{0:T(128)} %span_hbm.1, bf16[64,2048]{1,0:T(8,128)(2,1)} %q_hbm.1, bf16[64,2048]{1,0:T(8,128)(2,1)} %k_hbm.1, bf16[64,2048]{1,0:T(8,128)(2,1)} %v_hbm.1), custom_call_target="tpu_custom_call" | custom-call | tf_op jit(solution)/shard_map/pallas_call | solution.py:232
  1.9 28.8 %all_to_all.10 = bf16[32,49,2,128]{3,2,1,0:T(2,128)(2,1)S(1)} all-to-all(bf16[32,49,2,128]{3,2,1,0:T(2,128)(2,1)S(1)} %bitcast.5), channel_id=1, replica_groups={{0,16,24,8,10,26,18,2,1,17,25,9,11,27,19,3,4,20,28,12,14,30,22,6,5,21,2..., dimensions={0} | all-to-all | bytes 1605632 | tf_op jit(solution)/shard_map/all_to_all | solution.py:57
  30.7 0.2 shard_map.60
  30.9 0.1 collective-permute-start
  31.0 1.6 %shard_map.61 = (f32[1024,128]{1,0:T(8,128)S(1)}, f32[1024,128]{1,0:T(8,128)S(1)}, f32[1024,128]{1,0:T(8,128)S(1)}) custom-call(bf16[1024,128]{1,0:T(8,128)(2,1)S(1)} %get-tuple-element.7.query_ref, bf16[2112,128]{1,0:T(8,128)(2,1)S(1)} %get-tuple-element.8.mine_ref.other_ref, bf16[2112,128]{1,0:T(8,128)(2,1)S(1)} %get-tuple-element.8.mine_ref.other_ref), custom_call_target="tpu_custom_call" | custom-call | flops 536870912 | bytes 1048576 | tf_op jit(solution)/shard_map/pallas_call | solution.py:265
  32.5 0.3 collective-permute-done.other_ref
  32.9 1.7 %shard_map.62 = bf16[1088,128]{1,0:T(8,128)(2,1)S(1)} custom-call(bf16[1024,128]{1,0:T(8,128)(2,1)S(1)} %get-tuple-element.7.query_ref, bf16[2112,128]{1,0:T(8,128)(2,1)S(1)} %get-tuple-element.8.mine_ref.other_ref, bf16[2112,128]{1,0:T(8,128)(2,1)S(1)} %collective-permute-done.other_ref, f32[1024,128]{1,0:T(8,128)S(1)} %get-tuple-element.9.refs_0_, ...), custom_call_target="tpu_custom_call" | custom-call | flops 536870912 | bytes 1048576 | tf_op jit(solution)/shard_map/pallas_call | solution.py:265
  34.6 11.2 %all_to_all.11 = bf16[32,17,2,128]{3,2,1,0:T(2,128)(2,1)S(1)} all-to-all(bf16[32,17,2,128]{3,2,1,0:T(2,128)(2,1)S(1)} %bitcast.6), channel_id=1, replica_groups={{1,31,11,15,7,29,21,30,5,13,22,0,6,28,20,12,4,27,19,23,24,26,25,14,9,3,..., dimensions={0} | all-to-all | bytes 557056 | tf_op jit(solution)/shard_map/all_to_all | solution.py:57
  45.8 0.8 %shard_map.63 = (bf16[64,2048]{1,0:T(8,128)(2,1)}, f32[16,64]{1,0:T(8,128)}) custom-call(bf16[1088,128]{1,0:T(8,128)(2,1)S(1)} %bitcast.7), custom_call_target="tpu_custom_call" | custom-call | tf_op jit(solution)/shard_map/pallas_call | solution.py:279
Async XLA Ops:
  30.9 2.0 %collective-permute-start = (bf16[2112,128]{1,0:T(8,128)(2,1)S(1)}, bf16[2112,128]{1,0:T(8,128)(2,1)S(1)}, u32[]{:S(2)}, u32[]{:S(2)}) collective-permute-start(bf16[2112,128]{1,0:T(8,128)(2,1)S(1)} %get-tuple-element.8.mine_ref.other_ref), channel_id=1, source_target_pairs={{0,1},{1,0},{2,3},{3,2},{4,5},{5,4},{6,7},{7,6},{8,9},{9,8},{10,11... | collective-permute-start | bytes 1622024 | tf_op jit(solution)/shard_map/ppermute | solution.py:264

commit v10 on v9

--- a/solution.py
+++ b/solution.py
@@ -84,9 +84,9 @@
             ]
 
 
-def sort_kernel(in_ref, queries_ref, others_ref):
+def sort_kernel(in_ref, others_ref):
     for source in range(SOURCES):
-        for which, ref, start in ((1, others_ref, 0), (2, others_ref, KEYS), (0, queries_ref, 0)):
+        for which, ref, start in ((1, others_ref, 0), (2, others_ref, KEYS)):
             place = rows_of(source, SPAN, start, SPAN)
             ref[place, :] = in_ref[rows_of(source, THERE, which * SPAN, SPAN), :]
         place = rows_of(source, EXTRA, 2 * KEYS, EXTRA)
@@ -129,7 +129,7 @@
     def score(index):
         sources = range(index * GROUP, (index + 1) * GROUP)
         scores = lax.dot_general(
-            query_ref[index * block : (index + 1) * block, :],
+            jnp.concatenate([query_ref[rows_of(i, THERE, 0, SPAN), :] for i in sources], axis=0),
             keys,
             (((1,), (1,)), ((), ())),
             preferred_element_type=jnp.float32,
@@ -241,16 +241,14 @@
         ],
         compiler_params=params(),
     )(*in_hbm)
-    queries, mine = pl.pallas_call(
+    queries = exchanged(packed, THERE_ORDER)
+    mine = pl.pallas_call(
         sort_kernel,
-        out_shape=(
-            jax.ShapeDtypeStruct((KEYS, HEAD_DIM), jnp.bfloat16),
-            jax.ShapeDtypeStruct((2 * KEYS + SOURCES * EXTRA, HEAD_DIM), jnp.bfloat16),
-        ),
+        out_shape=jax.ShapeDtypeStruct((2 * KEYS + SOURCES * EXTRA, HEAD_DIM), jnp.bfloat16),
         in_specs=[VMEM],
-        out_specs=(VMEM, VMEM),
+        out_specs=VMEM,
         compiler_params=params(),
-    )(exchanged(packed, THERE_ORDER))
+    )(queries)
     ring = [(i, i // parts * parts + (i + 1) % parts) for i in range(devices)]
     state = ()
     other = mine

time: 47.1 us -> 47 us (level)
  no operation moved by 1% of the time
where the time goes in v10:
time: 47 us; the launch traced here: 46.5 us
  blocking collectives  40 us (85%)
  Pallas kernels  5.46 us (12%)
  between operations  0.66 us (1%)
    all_to_all x2, blocking collectives, exchanged(): lax.all_to_all(paired, 'source', 0, 0, axis_index_groups=groups, tiled=True)  40 us
    pallas_call x2, Pallas kernels, local(): pl.pallas_call(functools.partial(attend_kernel, first, last), out_shape=s...  3.33 us
    pallas_call x1, Pallas kernels, local(): pl.pallas_call(pack_kernel, out_shape=messages(THERE), in_specs=[HBM] * 4...  1.21 us
  transfers between devices with their start and end apart: 1, of which 1 were waited for; matrix products, arithmetic and copies ran while one was open for 0% of the time, Pallas kernels for 3%

profile of v10, /device:TPU:0, one launch (start us, length us, event | category | flops | bytes accessed | tf_op | source)
XLA Modules:
  0.0 46.5 jit_solution(18421479782792468974)
XLA Ops:
  0.6 1.2 %shard_map.59 = bf16[3136,128]{1,0:T(8,128)(2,1)S(1)} custom-call(s32[2]{0:T(128)} %span_hbm.1, bf16[64,2048]{1,0:T(8,128)(2,1)} %q_hbm.1, bf16[64,2048]{1,0:T(8,128)(2,1)} %k_hbm.1, bf16[64,2048]{1,0:T(8,128)(2,1)} %v_hbm.1), custom_call_target="tpu_custom_call" | custom-call | tf_op jit(solution)/shard_map/pallas_call | solution.py:232
  1.9 28.8 %all_to_all.10 = bf16[32,49,2,128]{3,2,1,0:T(2,128)(2,1)S(1)} all-to-all(bf16[32,49,2,128]{3,2,1,0:T(2,128)(2,1)S(1)} %bitcast.7), channel_id=1, replica_groups={{0,16,24,8,10,26,18,2,1,17,25,9,11,27,19,3,4,20,28,12,14,30,22,6,5,21,2..., dimensions={0} | all-to-all | bytes 1605632 | tf_op jit(solution)/shard_map/all_to_all | solution.py:57
  30.7 0.1 shard_map.60.mine_ref.other_ref
  30.8 0.1 collective-permute-start
  30.9 1.6 %shard_map.61 = (f32[1024,128]{1,0:T(8,128)S(1)}, f32[1024,128]{1,0:T(8,128)S(1)}, f32[1024,128]{1,0:T(8,128)S(1)}) custom-call(bf16[3136,128]{1,0:T(8,128)(2,1)S(1)} %bitcast.5, bf16[2112,128]{1,0:T(8,128)(2,1)S(1)} %shard_map.60.mine_ref.other_ref, bf16[2112,128]{1,0:T(8,128)(2,1)S(1)} %shard_map.60.mine_ref.other_ref), custom_call_target="tpu_custom_call" | custom-call | flops 536870912 | bytes 1048576 | tf_op jit(solution)/shard_map/pallas_call | solution.py:263
  32.5 0.3 collective-permute-done.other_ref
  32.8 1.7 %shard_map.62 = bf16[1088,128]{1,0:T(8,128)(2,1)S(1)} custom-call(bf16[3136,128]{1,0:T(8,128)(2,1)S(1)} %bitcast.6, bf16[2112,128]{1,0:T(8,128)(2,1)S(1)} %shard_map.60.mine_ref.other_ref, bf16[2112,128]{1,0:T(8,128)(2,1)S(1)} %collective-permute-done.other_ref, f32[1024,128]{1,0:T(8,128)S(1)} %get-tuple-element.5.refs_0_, ...), custom_call_target="tpu_custom_call" | custom-call | flops 536870912 | bytes 1048576 | tf_op jit(solution)/shard_map/pallas_call | solution.py:263
  34.6 11.2 %all_to_all.11 = bf16[32,17,2,128]{3,2,1,0:T(2,128)(2,1)S(1)} all-to-all(bf16[32,17,2,128]{3,2,1,0:T(2,128)(2,1)S(1)} %bitcast.8), channel_id=1, replica_groups={{1,31,11,15,7,29,21,30,5,13,22,0,6,28,20,12,4,27,19,23,24,26,25,14,9,3,..., dimensions={0} | all-to-all | bytes 557056 | tf_op jit(solution)/shard_map/all_to_all | solution.py:57
  45.7 0.8 %shard_map.63 = (bf16[64,2048]{1,0:T(8,128)(2,1)}, f32[16,64]{1,0:T(8,128)}) custom-call(bf16[1088,128]{1,0:T(8,128)(2,1)S(1)} %bitcast.9), custom_call_target="tpu_custom_call" | custom-call | tf_op jit(solution)/shard_map/pallas_call | solution.py:277
Async XLA Ops:
  30.8 2.0 %collective-permute-start = (bf16[2112,128]{1,0:T(8,128)(2,1)S(1)}, bf16[2112,128]{1,0:T(8,128)(2,1)S(1)}, u32[]{:S(2)}, u32[]{:S(2)}) collective-permute-start(bf16[2112,128]{1,0:T(8,128)(2,1)S(1)} %shard_map.60.mine_ref.other_ref), channel_id=1, source_target_pairs={{0,1},{1,0},{2,3},{3,2},{4,5},{5,4},{6,7},{7,6},{8,9},{9,8},{10,11... | collective-permute-start | bytes 1622024 | tf_op jit(solution)/shard_map/ppermute | solution.py:262
